TPU v7x, 32 devices: a whole 2x2x4 slice. The times are simulated.
32 devices in a mesh: groups: 2 (over y), expert: 16 (over z, x, core).
Axes of the slice: x: 2, y: 2, z: 4, core: 2. Of those that a mesh axis runs over, the one named last changes fastest.
Arguments:
- hidden_rows: bfloat16 [128, 7168], P(('groups', 'expert')), parts along dimension 0, may hold values from -6 to 6
- norm_gain: float32 [7168], replicated, may hold values from 0.1 to 1.9
- expert_ids: int32 [128, 2], P(('groups', 'expert')), parts along dimension 0, may hold values from 0 to 1, all different within a row; in each aligned block of 4 rows (0 to 3, 4 to 7, ...) at most 4 rows name the same one
- route_weights: float32 [128, 2], P(('groups', 'expert')), parts along dimension 0, may hold values from 0.05 to 0.5
- gate_weight: bfloat16 [16, 7168, 256], P('expert'), may hold values from -0.0625 to 0.0625
- up_weight: bfloat16 [16, 7168, 256], P('expert'), may hold values from -0.0625 to 0.0625
- down_weight: bfloat16 [16, 256, 7168], P('expert'), may hold values from -0.125 to 0.125
Outputs:
- expert_mix: bfloat16 [128, 7168], P(('groups', 'expert')), parts along dimension 0
There are 2 independent parts, one for each index of `groups`. A program takes and returns all parts, laid end to end along the dimension named above; an argument that names none is the same for every part. Nothing has to cross between parts.
Inputs may be any that keep to these rules, and one draw needn't show every extreme that they name: `expert_ids`: each row names 2 different experts; in each aligned block of 4 rows (the rows of one device) no expert is named by more than 4 rows, a bound that some block reaches.
All inputs are finite; a program needn't handle non-finite values.
Results may differ from a plain program's by a relative error of at most 0.0071.
Values may be sent and summed in bfloat16 or wider, within the bound.
No kernel may reach another device: no remote copies, remote signals or barrier semaphores. Data moves between devices by JAX's collectives and lax.ppermute only.
A program may use at most 128 MiB of HBM per device.

v0:
```python
import jax
import jax.numpy as jnp
from jax import lax
from jax.sharding import PartitionSpec as P

SHARDS = 8


def slot_select(member, slots):
    ranks = jnp.cumsum(member, axis=-1) - 1
    return (member[..., None, :] == 1) & (
        ranks[..., None, :] == jnp.arange(slots, dtype=jnp.int32)[:, None]
    )


def body(hidden_rows, norm_gain, expert_ids, route_weights, gate_weight, up_weight, down_weight):
    devices = lax.axis_size("expert")
    experts = devices // SHARDS
    tok_rows = hidden_rows.shape[0]
    width = hidden_rows.shape[1]
    top_count = expert_ids.shape[1]
    capacity = min(tok_rows, tok_rows * top_count // experts * 3 // 2)
    values = hidden_rows.astype(jnp.float32)
    scale = lax.rsqrt(jnp.mean(values * values, axis=-1, keepdims=True) + 1e-06)
    normed = (values * scale * norm_gain).astype(jnp.bfloat16)
    onehot = expert_ids[:, :, None] == jnp.arange(experts, dtype=jnp.int32)[None, None, :]
    member = jnp.any(onehot, axis=1).astype(jnp.int32)
    select = slot_select(member.T, capacity)
    packed = jnp.einsum(
        "ecr,rd->ecd", select.astype(jnp.bfloat16), normed, preferred_element_type=jnp.float32
    ).astype(jnp.bfloat16)
    weight_table = jnp.sum(route_weights[:, :, None] * onehot.astype(jnp.float32), axis=1)
    gate_piece = gate_weight[0]
    up_piece = up_weight[0]
    down_piece = down_weight[0]
    outgoing = jnp.repeat(packed, SHARDS, axis=0)
    received = lax.all_to_all(outgoing, "expert", split_axis=0, concat_axis=0, tiled=True)
    items = received.shape[1]
    rows = received.reshape(-1, width)
    gate = jnp.dot(rows, gate_piece, preferred_element_type=jnp.float32)
    upper = jnp.dot(rows, up_piece, preferred_element_type=jnp.float32)
    active = (jax.nn.silu(gate) * upper).astype(jnp.bfloat16)
    part = jnp.dot(active, down_piece, preferred_element_type=jnp.float32).astype(jnp.bfloat16)
    part = part.reshape(devices, items, width)
    back = lax.all_to_all(part, "expert", split_axis=0, concat_axis=0, tiled=True)
    summed = jnp.sum(back.astype(jnp.float32).reshape(experts, SHARDS, items, width), axis=1)
    combine = select.astype(jnp.float32).transpose(2, 0, 1) * weight_table[:, :, None]
    mixed = jnp.einsum("rec,ecd->rd", combine, summed, precision=lax.Precision.HIGHEST)
    return mixed.astype(jnp.bfloat16)


def solution(mesh):
    return jax.shard_map(
        body,
        mesh=mesh,
        in_specs=(
            P(("groups", "expert"), None),
            P(),
            P(("groups", "expert"), None),
            P(("groups", "expert"), None),
            P("expert", None, None),
            P("expert", None, None),
            P("expert", None, None),
        ),
        out_specs=P(("groups", "expert"), None),
        check_vma=False,
    )
```

profile of v0, /device:TPU:0, one launch (start us, length us, event | category | flops | bytes accessed | tf_op | source)
XLA Modules:
  0.0 69.6 jit_solution(1802015532733639937)
XLA Ops:
  0.0 0.7 fusion.36
  0.7 0.1 copy.15
  0.8 1.0 %fusion.14 = f32[4]{0:T(128)S(1)} fusion(bf16[4,7168]{1,0:T(4,128)(2,1)} %param.7), kind=kLoop, calls=%fused_computation.14 | loop fusion | flops 86012 | bytes 57360 | tf_op jit(solution)/shard_map/reduce_sum | solution.py:24
  1.8 0.1 copy.13
  2.0 0.1 copy.14
  2.1 1.1 %convolution_convert_fusion.1 = bf16[2,4,7168]{2,1,0:T(4,128)(2,1)S(1)} fusion(bf16[4,7168]{1,0:T(4,128)(2,1)} %param.7, f32[7168]{0:T(1024)} %param.8, f32[4]{0:T(128)S(1)} %add_rsqrt_fusion, s32[2,4]{1,0:T(2,128)S(1)} %copy.14, pred[2,4]{1,0:T(4,128)(4,1)S(1)} %copy.13), kind=kOutput, calls=%fused_computation.1 | convolution fusion | flops 630848 | bytes 200760 | tf_op jit(solution)/shard_map/ecr,rd->ecd/dot_general | solution.py:29
  3.1 0.2 broadcast_in_dim.2
  3.4 29.7 %all_to_all.10 = bf16[16,4,7168]{2,1,0:T(4,128)(2,1)S(1)} all-to-all(bf16[16,4,7168]{2,1,0:T(4,128)(2,1)S(1)} %bitcast.35), channel_id=1, replica_groups=mesh['groups'=2,'expert'=16] {'expert'}, dimensions={0} | all-to-all | bytes 1835008 | tf_op jit(solution)/shard_map/all_to_all | solution.py:37
  33.1 0.2 reshape.37
  33.3 2.8 %fusion.4 = f32[64,256]{1,0:T(8,128)S(1)} fusion(bf16[64,7168]{1,0:T(8,128)(2,1)S(1)} %reshape.37, bf16[1,7168,256]{2,1,0:T(8,128)(2,1)} %param.11), kind=kOutput, calls=%fused_computation.7 | convolution fusion | flops 234881024 | bytes 4653056 | tf_op jit(solution)/shard_map/dot_general | solution.py:40
  36.1 5.5 %convolution_convert_fusion = bf16[64,7168]{1,0:T(8,128)(2,1)S(1)} fusion(bf16[1,256,7168]{2,1,0:T(8,128)(2,1)} %param.13, bf16[64,7168]{1,0:T(8,128)(2,1)S(1)} %reshape.37, bf16[1,7168,256]{2,1,0:T(8,128)(2,1)} %param.12, f32[64,256]{1,0:T(8,128)S(1)} %fusion.4), kind=kOutput, calls=%fused_computation | convolution fusion | flops 470319104 | bytes 9240576 | tf_op jit(solution)/shard_map/dot_general | solution.py:43
  41.5 0.0 copy-start
  41.5 0.0 copy-start.1
  41.5 1.3 %reshape.38 = bf16[16,4,7168]{2,1,0:T(4,128)(2,1)} reshape(bf16[64,7168]{1,0:T(8,128)(2,1)S(1)} %convolution_convert_fusion) | data formatting | bytes 1835008 | tf_op jit(solution)/shard_map/reshape | solution.py:44
  42.8 4.5 %all-to-all-start.1 = ((bf16[16,4,7168]{2,1,0:T(4,128)(2,1)}), bf16[16,4,7168]{2,1,0:T(4,128)(2,1)S(1)}, u32[]{:S(2)}, u32[]{:S(2)}) async-start(bf16[16,4,7168]{2,1,0:T(4,128)(2,1)} %reshape.38), calls=%async_computation.1 | async-start | bytes 1835008 | tf_op jit(solution)/shard_map/all_to_all | solution.py:45
  47.3 0.1 copy.11
  47.4 0.1 copy.12
  47.5 0.0 copy-done
  47.5 0.0 copy-done.1
  47.5 20.6 %all-to-all-done.1 = bf16[16,4,7168]{2,1,0:T(4,128)(2,1)S(1)} async-done(((bf16[16,4,7168]{2,1,0:T(4,128)(2,1)}), bf16[16,4,7168]{2,1,0:T(4,128)(2,1)S(1)}, u32[]{:S(2)}, u32[]{:S(2)}) %all-to-all-start.1) | async-done | bytes 917536 | tf_op jit(solution)/shard_map/all_to_all | solution.py:45
  68.1 0.4 convert_reduce_fusion
  68.5 1.1 %fusion = bf16[4,7168]{1,0:T(4,128)(2,1)} fusion(f32[2,4,7168]{2,1,0:T(4,128)S(1)} %convert_reduce_fusion, f32[4,2]{0,1:T(2,128)S(1)} %select_reduce_fusion, s32[4,2]{0,1:T(2,128)S(1)} %copy.12, pred[4,2]{0,1:T(4,128)(4,1)S(1)} %copy.11), kind=kOutput, calls=%fused_computation.3 | convolution fusion | flops 2781280 | bytes 286792 | tf_op jit(solution)/shard_map/rec,ecd->rd/dot_general | solution.py:48
  (6 shorter events, 0.1 us)
Async XLA Ops:
  41.5 6.0 %copy-start = (s32[4,2]{0,1:T(2,128)S(1)}, s32[4,2]{0,1:T(2,128)}, u32[]{:S(2)}) copy-start(s32[4,2]{0,1:T(2,128)} %param.9) | copy-start | bytes 100
  41.5 6.0 %copy-start.1 = (f32[4,2]{0,1:T(2,128)S(1)}, f32[4,2]{0,1:T(2,128)}, u32[]{:S(2)}) copy-start(f32[4,2]{0,1:T(2,128)} %param.10) | copy-start | bytes 100
  42.8 25.3 %all-to-all-start.1 = ((bf16[16,4,7168]{2,1,0:T(4,128)(2,1)}), bf16[16,4,7168]{2,1,0:T(4,128)(2,1)S(1)}, u32[]{:S(2)}, u32[]{:S(2)}) async-start(bf16[16,4,7168]{2,1,0:T(4,128)(2,1)} %reshape.38), calls=%async_computation.1 | async-start | bytes 1835008 | tf_op jit(solution)/shard_map/all_to_all | solution.py:45
where the time goes:
time: 70.6 us; the launch traced here: 69.6 us
  blocking collectives  29.7 us (42%)
  waiting for transfers between devices  20.6 us (29%)
  matrix products  10.4 us (15%)
  starting transfers between devices  4.48 us (6%)
  local copies, waits for them, and re-layouts  2.23 us (3%)
  other arithmetic  2.16 us (3%)
    all_to_all x1, blocking collectives, body(): lax.all_to_all(outgoing, 'expert', split_axis=0, concat_axis=0, tiled=True)  29.7 us
    all_to_all x1, waiting for transfers between devices, body(): lax.all_to_all(part, 'expert', split_axis=0, concat_axis=0, tiled=True)  20.6 us
    dot_general x1, matrix products, body(): jnp.dot(active, down_piece, preferred_element_type=jnp.float32)  5.45 us
    all_to_all x1, starting transfers between devices, body(): lax.all_to_all(part, 'expert', split_axis=0, concat_axis=0, tiled=True)  4.48 us
    dot_general x1, matrix products, body(): gate = jnp.dot(rows, gate_piece, preferred_element_type=jnp.float32)  2.75 us
  transfers between devices with their start and end apart: 1, of which 1 were waited for; matrix products, arithmetic and copies ran while one was open for 0% of the time, Pallas kernels for 0%

commit v1 on v0

--- a/solution.py
+++ b/solution.py
@@ -1,9 +1,17 @@
+import functools
+
 import jax
 import jax.numpy as jnp
 from jax import lax
+from jax.experimental import pallas as pl
+from jax.experimental.pallas import tpu as pltpu
 from jax.sharding import PartitionSpec as P
 
 SHARDS = 8
+CHUNKS = 4
+VMEM = pl.BlockSpec(memory_space=pltpu.VMEM)
+ANY = pl.BlockSpec(memory_space=pl.ANY)
+SMALL = pltpu.CompilerParams(vmem_limit_bytes=4 * 1024 * 1024)
 
 
 def slot_select(member, slots):
@@ -13,7 +21,7 @@
     )
 
 
-def body(hidden_rows, norm_gain, expert_ids, route_weights, gate_weight, up_weight, down_weight):
+def routed_body(hidden_rows, norm_gain, expert_ids, route_weights, gate_weight, up_weight, down_weight):
     devices = lax.axis_size("expert")
     experts = devices // SHARDS
     tok_rows = hidden_rows.shape[0]
@@ -49,6 +57,143 @@
     return mixed.astype(jnp.bfloat16)
 
 
+def swap(array, mask):
+    devices = lax.axis_size("expert")
+    return lax.ppermute(array, "expert", [(i, i ^ mask) for i in range(devices)])
+
+
+def expert_kernel(count, *refs):
+    pieces = refs[:count]
+    gain, gate_hbm, up_hbm, down_hbm = refs[count : count + 4]
+    keep, give = refs[count + 4 : count + 6]
+    normed, gate_w, up_w, down_w, gate_sem, up_sem, down_sem = refs[count + 6 :]
+    tok, width = pieces[0].shape
+    step = width // CHUNKS
+    copies = []
+    for c in range(CHUNKS):
+        part = pl.ds(c * step, step)
+        copies.append(
+            (
+                pltpu.make_async_copy(gate_hbm.at[0, part], gate_w.at[part], gate_sem.at[c]),
+                pltpu.make_async_copy(up_hbm.at[0, part], up_w.at[part], up_sem.at[c]),
+            )
+        )
+    downs = []
+    for c in range(CHUNKS):
+        part = pl.ds(c * step, step)
+        downs.append(pltpu.make_async_copy(down_hbm.at[0, :, part], down_w.at[:, part], down_sem.at[c]))
+    for pair in copies:
+        pair[0].start()
+        pair[1].start()
+    for copy in downs:
+        copy.start()
+    for k in range(count):
+        values = pieces[k][...].astype(jnp.float32)
+        scale = lax.rsqrt(jnp.mean(values * values, axis=-1, keepdims=True) + 1e-06)
+        normed[tok * k : tok * (k + 1), :] = (values * scale * gain[...]).astype(jnp.bfloat16)
+    gate = jnp.zeros((tok * count, gate_w.shape[1]), jnp.float32)
+    upper = gate
+    for c in range(CHUNKS):
+        copies[c][0].wait()
+        copies[c][1].wait()
+        part = slice(c * step, (c + 1) * step)
+        rows = normed[:, part]
+        gate = gate + jnp.dot(rows, gate_w[part, :], preferred_element_type=jnp.float32)
+        upper = upper + jnp.dot(rows, up_w[part, :], preferred_element_type=jnp.float32)
+    active = (gate / (1.0 + jnp.exp(-gate)) * upper).astype(jnp.bfloat16)
+    for c in range(CHUNKS):
+        downs[c].wait()
+        part = slice(c * step, (c + 1) * step)
+        result = jnp.dot(active, down_w[:, part], preferred_element_type=jnp.float32)
+        for k in range(count):
+            block = result[tok * k : tok * (k + 1)].astype(jnp.bfloat16)
+            if k % 2 == 0:
+                keep[k // 2, :, part] = block
+            else:
+                give[k // 2, :, part] = block
+
+
+def experts_call(pieces, gain, gate_weight, up_weight, down_weight):
+    count = len(pieces)
+    tok, width = pieces[0].shape
+    units = gate_weight.shape[2]
+    half = jax.ShapeDtypeStruct((count // 2, tok, width), jnp.bfloat16)
+    return pl.pallas_call(
+        functools.partial(expert_kernel, count),
+        out_shape=(half, half),
+        in_specs=[VMEM] * (count + 1) + [ANY] * 3,
+        out_specs=(VMEM, VMEM),
+        scratch_shapes=[
+            pltpu.VMEM((tok * count, width), jnp.bfloat16),
+            pltpu.VMEM((width, units), jnp.bfloat16),
+            pltpu.VMEM((width, units), jnp.bfloat16),
+            pltpu.VMEM((units, width), jnp.bfloat16),
+            pltpu.SemaphoreType.DMA((CHUNKS,)),
+            pltpu.SemaphoreType.DMA((CHUNKS,)),
+            pltpu.SemaphoreType.DMA((CHUNKS,)),
+        ],
+        compiler_params=pltpu.CompilerParams(vmem_limit_bytes=57 * 1024 * 1024),
+    )(*pieces, gain, gate_weight, up_weight, down_weight)
+
+
+def pair_kernel(keep, got, *outs):
+    for i, out in enumerate(outs):
+        out[...] = (keep[i + 1].astype(jnp.float32) + got[i + 1].astype(jnp.float32)).astype(jnp.bfloat16)
+
+
+def sum_kernel(*refs):
+    total = refs[0][...].astype(jnp.float32)
+    for ref in refs[1:-1]:
+        total = total + ref[...].astype(jnp.float32)
+    refs[-1][...] = total.astype(jnp.bfloat16)
+
+
+def last_kernel(tables, keep, got, a, b, c, cross, out):
+    own = keep[0].astype(jnp.float32) + got[0].astype(jnp.float32)
+    own = own + a[...].astype(jnp.float32) + b[...].astype(jnp.float32) + c[...].astype(jnp.float32)
+    weight = tables[...]
+    out[...] = (weight[:, 0:1] * own + weight[:, 1:2] * cross[...].astype(jnp.float32)).astype(jnp.bfloat16)
+
+
+def dense_body(hidden_rows, norm_gain, expert_ids, route_weights, gate_weight, up_weight, down_weight):
+    own_expert = lax.axis_index("expert") // SHARDS
+    ids = jnp.stack([own_expert, 1 - own_expert]).astype(jnp.int32)
+    table = jnp.sum(
+        jnp.where(expert_ids[:, :, None] == ids[None, None, :], route_weights[:, :, None], 0.0), axis=1
+    )
+    x = hidden_rows
+    piece = {0: x}
+    piece[8] = swap(x, 8)
+    for k in (2, 4, 6):
+        piece[k] = swap(x, k)
+    for k in (2, 4, 6):
+        piece[8 + k] = swap(piece[8], k)
+    for k in range(0, 16, 2):
+        piece[k + 1] = swap(piece[k], 1)
+    keep, give = experts_call(
+        [piece[k] for k in range(16)], norm_gain[None, :], gate_weight, up_weight, down_weight
+    )
+    got = swap(give, 1)
+    block = jax.ShapeDtypeStruct(x.shape, jnp.bfloat16)
+    sums = pl.pallas_call(pair_kernel, out_shape=(block,) * 7, in_specs=[VMEM] * 2, out_specs=(VMEM,) * 7, compiler_params=SMALL)(keep, got)
+    sums = {2 * (i + 1): s for i, s in enumerate(sums)}
+    far = [swap(sums[8 + k], k) for k in (2, 4, 6)]
+    across = pl.pallas_call(sum_kernel, out_shape=block, in_specs=[VMEM] * 4, out_specs=VMEM, compiler_params=SMALL)(sums[8], *far)
+    cross = swap(across, 8)
+    near = [swap(sums[k], k) for k in (2, 4, 6)]
+    return pl.pallas_call(last_kernel, out_shape=block, in_specs=[VMEM] * 7, out_specs=VMEM, compiler_params=SMALL)(
+        table, keep, got, *near, cross
+    )
+
+
+def body(*args):
+    devices = lax.axis_size("expert")
+    experts = devices // SHARDS
+    if experts == 2 and args[2].shape[1] == 2:
+        return dense_body(*args)
+    return routed_body(*args)
+
+
 def solution(mesh):
     return jax.shard_map(
         body,

time: 70.6 us -> 43.6 us (0.62)
  blocking collectives: 29.7 us -> 0 us
  starting transfers between devices: 4.48 us -> 22.9 us
  waiting for transfers between devices: 20.6 us -> 8.69 us
  matrix products: 10.4 us -> 0 us
  Pallas kernels: 0 us -> 8.76 us
  other arithmetic: 2.16 us -> 0.15 us
    all_to_all x1 -> x0, blocking collectives: 29.7 us -> none  [body(): lax.all_to_all(outgoing, 'expert', split_axis=0, concat_axis=0, tiled=True)]
    ppermute x0 -> x23, starting transfers between devices: none -> 22.9 us  [swap(): lax.ppermute(array, 'expert', [(i, i ^ mask) for i in range(devices)])]
    all_to_all x1 -> x0, waiting for transfers between devices: 20.6 us -> none  [body(): lax.all_to_all(part, 'expert', split_axis=0, concat_axis=0, tiled=True)]
    dot_general x4 -> x0, matrix products: 10.4 us -> none  [the longest x1 5.45 us: body(): jnp.dot(active, down_piece, preferred_element_type=jnp.float32)]
    pallas_call x0 -> x4, Pallas kernels: none -> 8.76 us  [the longest x1 7.81 us: experts_call(): pl.pallas_call(functools.partial(expert_kernel, count), out_shape=(half,...]
    ppermute x0 -> x23, waiting for transfers between devices: none -> 8.69 us  [swap(): lax.ppermute(array, 'expert', [(i, i ^ mask) for i in range(devices)])]
    all_to_all x1 -> x0, starting transfers between devices: 4.48 us -> none  [body(): lax.all_to_all(part, 'expert', split_axis=0, concat_axis=0, tiled=True)]
    unnamed x5 -> x38, local copies, waits for them, and re-layouts: 0.12 us -> 2.6 us
  transfers between devices with their start and end apart: 1 -> 23, of which waited for: 1 -> 8; matrix products, arithmetic and copies ran while one was open for 0% -> 1% of each run, Pallas kernels for 0% -> 0%
where the time goes in v1:
time: 43.6 us; the launch traced here: 43.3 us
  starting transfers between devices  22.9 us (53%)
  Pallas kernels  8.76 us (20%)
  waiting for transfers between devices  8.69 us (20%)
  local copies, waits for them, and re-layouts  2.7 us (6%)
    ppermute x23, starting transfers between devices, swap(): lax.ppermute(array, 'expert', [(i, i ^ mask) for i in range(devices)])  22.9 us
    ppermute x23, waiting for transfers between devices, swap(): lax.ppermute(array, 'expert', [(i, i ^ mask) for i in range(devices)])  8.69 us
    pallas_call x1, Pallas kernels, experts_call(): pl.pallas_call(functools.partial(expert_kernel, count), out_shape=(half,...  7.81 us
    unnamed x38, local copies, waits for them, and re-layouts  2.6 us
  transfers between devices with their start and end apart: 23, of which 8 were waited for; matrix products, arithmetic and copies ran while one was open for 1% of the time, Pallas kernels for 0%

profile of v1, /device:TPU:0, one launch (start us, length us, event | category | flops | bytes accessed | tf_op | source)
XLA Modules:
  0.0 43.3 jit_solution(12931264367060970127)
XLA Ops:
  0.0 4.0 %collective-permute-start.7 = (bf16[4,7168]{1,0:T(4,128)(2,1)}, bf16[4,7168]{1,0:T(4,128)(2,1)S(1)}, u32[]{:S(2)}, u32[]{:S(2)}) collective-permute-start(bf16[4,7168]{1,0:T(4,128)(2,1)} %refs_0_.1), channel_id=1, source_target_pairs={{0,8},{1,9},{2,10},{3,11},{4,12},{5,13},{6,14},{7,15},{8,0},{9,1},... | collective-permute-start | bytes 172040 | tf_op jit(solution)/shard_map/ppermute | solution.py:62
  4.0 1.5 %collective-permute-start.1 = (bf16[4,7168]{1,0:T(4,128)(2,1)}, bf16[4,7168]{1,0:T(4,128)(2,1)S(1)}, u32[]{:S(2)}, u32[]{:S(2)}) collective-permute-start(bf16[4,7168]{1,0:T(4,128)(2,1)} %refs_0_.1), channel_id=1, source_target_pairs={{0,2},{1,3},{2,0},{3,1},{4,6},{5,7},{6,4},{7,5},{8,10},{9,11},{10,... | collective-permute-start | bytes 172040 | tf_op jit(solution)/shard_map/ppermute | solution.py:62
  5.5 1.6 %collective-permute-start.3 = (bf16[4,7168]{1,0:T(4,128)(2,1)}, bf16[4,7168]{1,0:T(4,128)(2,1)S(1)}, u32[]{:S(2)}, u32[]{:S(2)}) collective-permute-start(bf16[4,7168]{1,0:T(4,128)(2,1)} %refs_0_.1), channel_id=1, source_target_pairs={{0,4},{1,5},{2,6},{3,7},{4,0},{5,1},{6,2},{7,3},{8,12},{9,13},{10,... | collective-permute-start | bytes 172040 | tf_op jit(solution)/shard_map/ppermute | solution.py:62
  7.1 0.4 collective-permute-start.5
  7.5 0.0 collective-permute-start
  7.5 0.0 collective-permute-done.7.refs_8_
  7.5 1.6 %collective-permute-start.9 = (bf16[4,7168]{1,0:T(4,128)(2,1)S(1)}, bf16[4,7168]{1,0:T(4,128)(2,1)S(1)}, u32[]{:S(2)}, u32[]{:S(2)}) collective-permute-start(bf16[4,7168]{1,0:T(4,128)(2,1)S(1)} %collective-permute-done.7.refs_8_), channel_id=1, source_target_pairs={{0,2},{1,3},{2,0},{3,1},{4,6},{5,7},{6,4},{7,5},{8,10},{9,11},{10,... | collective-permute-start | bytes 172040 | tf_op jit(solution)/shard_map/ppermute | solution.py:62
  9.1 0.0 collective-permute-done.1.refs_2_
  9.1 1.6 %collective-permute-start.11 = (bf16[4,7168]{1,0:T(4,128)(2,1)S(1)}, bf16[4,7168]{1,0:T(4,128)(2,1)S(1)}, u32[]{:S(2)}, u32[]{:S(2)}) collective-permute-start(bf16[4,7168]{1,0:T(4,128)(2,1)S(1)} %collective-permute-done.7.refs_8_), channel_id=1, source_target_pairs={{0,4},{1,5},{2,6},{3,7},{4,0},{5,1},{6,2},{7,3},{8,12},{9,13},{10,... | collective-permute-start | bytes 172040 | tf_op jit(solution)/shard_map/ppermute | solution.py:62
  10.7 0.0 collective-permute-done.3.refs_4_
  10.7 0.9 %collective-permute-start.13 = (bf16[4,7168]{1,0:T(4,128)(2,1)S(1)}, bf16[4,7168]{1,0:T(4,128)(2,1)S(1)}, u32[]{:S(2)}, u32[]{:S(2)}) collective-permute-start(bf16[4,7168]{1,0:T(4,128)(2,1)S(1)} %collective-permute-done.7.refs_8_), channel_id=1, source_target_pairs={{0,6},{1,7},{2,4},{3,5},{4,2},{5,3},{6,0},{7,1},{8,14},{9,15},{10,... | collective-permute-start | bytes 172040 | tf_op jit(solution)/shard_map/ppermute | solution.py:62
  11.6 1.3 %collective-permute-done.5.refs_6_ = bf16[4,7168]{1,0:T(4,128)(2,1)S(1)} collective-permute-done((bf16[4,7168]{1,0:T(4,128)(2,1)}, bf16[4,7168]{1,0:T(4,128)(2,1)S(1)}, u32[]{:S(2)}, u32[]{:S(2)}) %collective-permute-start.5) | collective-permute-done | bytes 57376 | tf_op jit(solution)/shard_map/ppermute | solution.py:62
  13.0 0.0 collective-permute-start.8
  13.0 0.0 collective-permute-done.refs_1_
  13.0 0.0 copy-start.6
  13.0 0.5 %collective-permute-start.2 = (bf16[4,7168]{1,0:T(4,128)(2,1)S(1)}, bf16[4,7168]{1,0:T(4,128)(2,1)S(1)}, u32[]{:S(2)}, u32[]{:S(2)}) collective-permute-start(bf16[4,7168]{1,0:T(4,128)(2,1)S(1)} %collective-permute-done.1.refs_2_), channel_id=1, source_target_pairs={{0,1},{1,0},{2,3},{3,2},{4,5},{5,4},{6,7},{7,6},{8,9},{9,8},{10,11... | collective-permute-start | bytes 172040 | tf_op jit(solution)/shard_map/ppermute | solution.py:62
  13.5 0.0 collective-permute-done.9.refs_10_
  13.5 0.1 collective-permute-start.4
  13.6 0.0 collective-permute-done.11.refs_12_
  13.6 0.4 collective-permute-start.6
  14.0 1.8 %collective-permute-done.13.refs_14_ = bf16[4,7168]{1,0:T(4,128)(2,1)S(1)} collective-permute-done((bf16[4,7168]{1,0:T(4,128)(2,1)S(1)}, bf16[4,7168]{1,0:T(4,128)(2,1)S(1)}, u32[]{:S(2)}, u32[]{:S(2)}) %collective-permute-start.13) | collective-permute-done | bytes 57376 | tf_op jit(solution)/shard_map/ppermute | solution.py:62
  15.8 0.0 collective-permute-start.10
  15.8 0.0 collective-permute-done.8.refs_9_
  15.8 0.0 copy-start.10
  15.8 0.5 %collective-permute-start.12 = (bf16[4,7168]{1,0:T(4,128)(2,1)S(1)}, bf16[4,7168]{1,0:T(4,128)(2,1)S(1)}, u32[]{:S(2)}, u32[]{:S(2)}) collective-permute-start(bf16[4,7168]{1,0:T(4,128)(2,1)S(1)} %collective-permute-done.11.refs_12_), channel_id=1, source_target_pairs={{0,1},{1,0},{2,3},{3,2},{4,5},{5,4},{6,7},{7,6},{8,9},{9,8},{10,11... | collective-permute-start | bytes 172040 | tf_op jit(solution)/shard_map/ppermute | solution.py:62
  16.3 0.0 collective-permute-done.2.refs_3_
  16.3 0.1 collective-permute-start.14
  16.4 0.0 collective-permute-done.4.refs_5_
  16.4 0.0 collective-permute-done.6.refs_7_
  16.4 0.0 copy-start.13
  16.4 0.6 %collective-permute-done.10.refs_11_ = bf16[4,7168]{1,0:T(4,128)(2,1)S(1)} collective-permute-done((bf16[4,7168]{1,0:T(4,128)(2,1)S(1)}, bf16[4,7168]{1,0:T(4,128)(2,1)S(1)}, u32[]{:S(2)}, u32[]{:S(2)}) %collective-permute-start.10) | collective-permute-done | bytes 57376 | tf_op jit(solution)/shard_map/ppermute | solution.py:62
  17.0 0.2 collective-permute-done.12.refs_13_
  17.2 0.4 collective-permute-done.14.refs_15_
  17.5 0.0 copy-done.2
  17.5 0.0 copy-done.3
  17.5 0.0 copy-done.4
  17.5 0.0 copy-done.5
  17.6 0.1 copy-done.15
  17.8 0.4 copy-done.16
  18.1 7.8 %shard_map.73 = (bf16[8,4,7168]{2,1,0:T(4,128)(2,1)}, bf16[8,4,7168]{2,1,0:T(4,128)(2,1)}) custom-call(bf16[4,7168]{1,0:T(4,128)(2,1)} %refs_0_.1, bf16[4,7168]{1,0:T(4,128)(2,1)} %copy-done.6, bf16[4,7168]{1,0:T(4,128)(2,1)} %copy-done.3, bf16[4,7168]{1,0:T(4,128)(2,1)} %copy-done.11, bf16[4,7168]{1,0:T(4,128)(2,1)} %copy-done.4, ...), custom_call_target="tpu_custom_call" | custom-call | tf_op jit(solution)/shard_map/pallas_call | solution.py:121
  26.0 0.2 collective-permute-start.15
  26.2 1.9 %collective-permute-done.15.got = bf16[8,4,7168]{2,1,0:T(4,128)(2,1)S(1)} collective-permute-done((bf16[8,4,7168]{2,1,0:T(4,128)(2,1)}, bf16[8,4,7168]{2,1,0:T(4,128)(2,1)S(1)}, u32[]{:S(2)}, u32[]{:S(2)}) %collective-permute-start.15) | collective-permute-done | bytes 458784 | tf_op jit(solution)/shard_map/ppermute | solution.py:62
  28.1 1.0 %copy-done = bf16[8,4,7168]{2,1,0:T(4,128)(2,1)S(1)} copy-done((bf16[8,4,7168]{2,1,0:T(4,128)(2,1)S(1)}, bf16[8,4,7168]{2,1,0:T(4,128)(2,1)}, u32[]{:S(2)}) %copy-start) | copy-done | bytes 458776
  29.1 0.2 shard_map.74
  29.3 1.5 %collective-permute-start.19 = (bf16[4,7168]{1,0:T(4,128)(2,1)S(1)}, bf16[4,7168]{1,0:T(4,128)(2,1)S(1)}, u32[]{:S(2)}, u32[]{:S(2)}) collective-permute-start(bf16[4,7168]{1,0:T(4,128)(2,1)S(1)} %get-tuple-element.20), channel_id=1, source_target_pairs={{0,2},{1,3},{2,0},{3,1},{4,6},{5,7},{6,4},{7,5},{8,10},{9,11},{10,... | collective-permute-start | bytes 172040 | tf_op jit(solution)/shard_map/ppermute | solution.py:62
  30.8 0.2 collective-permute-start.20
  30.9 1.9 %collective-permute-start.21 = (bf16[4,7168]{1,0:T(4,128)(2,1)S(1)}, bf16[4,7168]{1,0:T(4,128)(2,1)S(1)}, u32[]{:S(2)}, u32[]{:S(2)}) collective-permute-start(bf16[4,7168]{1,0:T(4,128)(2,1)S(1)} %get-tuple-element.22), channel_id=1, source_target_pairs={{0,6},{1,7},{2,4},{3,5},{4,2},{5,3},{6,0},{7,1},{8,14},{9,15},{10,... | collective-permute-start | bytes 172040 | tf_op jit(solution)/shard_map/ppermute | solution.py:62
  32.8 0.1 pad_add_fusion
  32.9 1.4 %collective-permute-start.16 = (bf16[4,7168]{1,0:T(4,128)(2,1)S(1)}, bf16[4,7168]{1,0:T(4,128)(2,1)S(1)}, u32[]{:S(2)}, u32[]{:S(2)}) collective-permute-start(bf16[4,7168]{1,0:T(4,128)(2,1)S(1)} %get-tuple-element.16), channel_id=1, source_target_pairs={{0,2},{1,3},{2,0},{3,1},{4,6},{5,7},{6,4},{7,5},{8,10},{9,11},{10,... | collective-permute-start | bytes 172040 | tf_op jit(solution)/shard_map/ppermute | solution.py:62
  34.3 0.2 collective-permute-start.17
  34.5 0.0 collective-permute-done.19.refs_1_
  34.5 1.9 %collective-permute-start.18 = (bf16[4,7168]{1,0:T(4,128)(2,1)S(1)}, bf16[4,7168]{1,0:T(4,128)(2,1)S(1)}, u32[]{:S(2)}, u32[]{:S(2)}) collective-permute-start(bf16[4,7168]{1,0:T(4,128)(2,1)S(1)} %get-tuple-element.18), channel_id=1, source_target_pairs={{0,6},{1,7},{2,4},{3,5},{4,2},{5,3},{6,0},{7,1},{8,14},{9,15},{10,... | collective-permute-start | bytes 172040 | tf_op jit(solution)/shard_map/ppermute | solution.py:62
  36.4 0.0 collective-permute-done.20.refs_2_
  36.4 0.0 collective-permute-done.21.refs_3_
  36.4 2.4 %collective-permute-start.22 = (bf16[4,7168]{1,0:T(4,128)(2,1)S(1)}, bf16[4,7168]{1,0:T(4,128)(2,1)S(1)}, u32[]{:S(2)}, u32[]{:S(2)}) collective-permute-start(bf16[4,7168]{1,0:T(4,128)(2,1)S(1)} %shard_map.75), channel_id=1, source_target_pairs={{0,8},{1,9},{2,10},{3,11},{4,12},{5,13},{6,14},{7,15},{8,0},{9,1},... | collective-permute-start | bytes 172040 | tf_op jit(solution)/shard_map/ppermute | solution.py:62
  38.8 0.0 copy-done.18
  38.8 0.1 fusion
  38.9 0.1 copy.10.tables
  39.0 0.0 collective-permute-done.16.a
  39.0 0.0 collective-permute-done.17.b
  39.0 0.8 %collective-permute-done.18.c = bf16[4,7168]{1,0:T(4,128)(2,1)S(1)} collective-permute-done((bf16[4,7168]{1,0:T(4,128)(2,1)S(1)}, bf16[4,7168]{1,0:T(4,128)(2,1)S(1)}, u32[]{:S(2)}, u32[]{:S(2)}) %collective-permute-start.18) | collective-permute-done | bytes 57376 | tf_op jit(solution)/shard_map/ppermute | solution.py:62
  39.8 1.7 %collective-permute-done.22.cross = bf16[4,7168]{1,0:T(4,128)(2,1)S(1)} collective-permute-done((bf16[4,7168]{1,0:T(4,128)(2,1)S(1)}, bf16[4,7168]{1,0:T(4,128)(2,1)S(1)}, u32[]{:S(2)}, u32[]{:S(2)}) %collective-permute-start.22) | collective-permute-done | bytes 57376 | tf_op jit(solution)/shard_map/ppermute | solution.py:62
  41.6 1.0 %copy-done.1 = bf16[8,4,7168]{2,1,0:T(4,128)(2,1)S(1)} copy-done((bf16[8,4,7168]{2,1,0:T(4,128)(2,1)S(1)}, bf16[8,4,7168]{2,1,0:T(4,128)(2,1)}, u32[]{:S(2)}) %copy-start.1) | copy-done | bytes 458776
  42.6 0.7 %shard_map.76 = bf16[4,7168]{1,0:T(4,128)(2,1)} custom-call(f32[4,2]{1,0:T(4,128)S(1)} %copy.10.tables, bf16[8,4,7168]{2,1,0:T(4,128)(2,1)S(1)} %copy-done.1, bf16[8,4,7168]{2,1,0:T(4,128)(2,1)S(1)} %collective-permute-done.15.got, bf16[4,7168]{1,0:T(4,128)(2,1)S(1)} %collective-permute-done.16.a, bf16[4,7168]{1,0:T(4,128)(2,1)S(1)} %collective-permute-done.17.b, ...), custom_call_target="tpu_custom_call" | custom-call | tf_op jit(solution)/shard_map/pallas_call | solution.py:184
  (27 shorter events, 0.1 us)
Async XLA Ops:
  0.0 7.5 %collective-permute-start.7 = (bf16[4,7168]{1,0:T(4,128)(2,1)}, bf16[4,7168]{1,0:T(4,128)(2,1)S(1)}, u32[]{:S(2)}, u32[]{:S(2)}) collective-permute-start(bf16[4,7168]{1,0:T(4,128)(2,1)} %refs_0_.1), channel_id=1, source_target_pairs={{0,8},{1,9},{2,10},{3,11},{4,12},{5,13},{6,14},{7,15},{8,0},{9,1},... | collective-permute-start | bytes 172040 | tf_op jit(solution)/shard_map/ppermute | solution.py:62
  4.0 5.1 %collective-permute-start.1 = (bf16[4,7168]{1,0:T(4,128)(2,1)}, bf16[4,7168]{1,0:T(4,128)(2,1)S(1)}, u32[]{:S(2)}, u32[]{:S(2)}) collective-permute-start(bf16[4,7168]{1,0:T(4,128)(2,1)} %refs_0_.1), channel_id=1, source_target_pairs={{0,2},{1,3},{2,0},{3,1},{4,6},{5,7},{6,4},{7,5},{8,10},{9,11},{10,... | collective-permute-start | bytes 172040 | tf_op jit(solution)/shard_map/ppermute | solution.py:62
  5.5 5.2 %collective-permute-start.3 = (bf16[4,7168]{1,0:T(4,128)(2,1)}, bf16[4,7168]{1,0:T(4,128)(2,1)S(1)}, u32[]{:S(2)}, u32[]{:S(2)}) collective-permute-start(bf16[4,7168]{1,0:T(4,128)(2,1)} %refs_0_.1), channel_id=1, source_target_pairs={{0,4},{1,5},{2,6},{3,7},{4,0},{5,1},{6,2},{7,3},{8,12},{9,13},{10,... | collective-permute-start | bytes 172040 | tf_op jit(solution)/shard_map/ppermute | solution.py:62
  7.1 5.9 %collective-permute-start.5 = (bf16[4,7168]{1,0:T(4,128)(2,1)}, bf16[4,7168]{1,0:T(4,128)(2,1)S(1)}, u32[]{:S(2)}, u32[]{:S(2)}) collective-permute-start(bf16[4,7168]{1,0:T(4,128)(2,1)} %refs_0_.1), channel_id=1, source_target_pairs={{0,6},{1,7},{2,4},{3,5},{4,2},{5,3},{6,0},{7,1},{8,14},{9,15},{10,... | collective-permute-start | bytes 172040 | tf_op jit(solution)/shard_map/ppermute | solution.py:62
  7.5 5.4 %collective-permute-start = (bf16[4,7168]{1,0:T(4,128)(2,1)}, bf16[4,7168]{1,0:T(4,128)(2,1)S(1)}, u32[]{:S(2)}, u32[]{:S(2)}) collective-permute-start(bf16[4,7168]{1,0:T(4,128)(2,1)} %refs_0_.1), channel_id=1, source_target_pairs={{0,1},{1,0},{2,3},{3,2},{4,5},{5,4},{6,7},{7,6},{8,9},{9,8},{10,11... | collective-permute-start | bytes 172040 | tf_op jit(solution)/shard_map/ppermute | solution.py:62
  7.5 10.0 %copy-start.2 = (bf16[4,7168]{1,0:T(4,128)(2,1)}, bf16[4,7168]{1,0:T(4,128)(2,1)S(1)}, u32[]{:S(2)}) copy-start(bf16[4,7168]{1,0:T(4,128)(2,1)S(1)} %collective-permute-done.7.refs_8_) | copy-start | bytes 172036
  7.5 5.9 %collective-permute-start.9 = (bf16[4,7168]{1,0:T(4,128)(2,1)S(1)}, bf16[4,7168]{1,0:T(4,128)(2,1)S(1)}, u32[]{:S(2)}, u32[]{:S(2)}) collective-permute-start(bf16[4,7168]{1,0:T(4,128)(2,1)S(1)} %collective-permute-done.7.refs_8_), channel_id=1, source_target_pairs={{0,2},{1,3},{2,0},{3,1},{4,6},{5,7},{6,4},{7,5},{8,10},{9,11},{10,... | collective-permute-start | bytes 172040 | tf_op jit(solution)/shard_map/ppermute | solution.py:62
  9.1 8.4 %copy-start.3 = (bf16[4,7168]{1,0:T(4,128)(2,1)}, bf16[4,7168]{1,0:T(4,128)(2,1)S(1)}, u32[]{:S(2)}) copy-start(bf16[4,7168]{1,0:T(4,128)(2,1)S(1)} %collective-permute-done.1.refs_2_) | copy-start | bytes 172036
  9.1 4.5 %collective-permute-start.11 = (bf16[4,7168]{1,0:T(4,128)(2,1)S(1)}, bf16[4,7168]{1,0:T(4,128)(2,1)S(1)}, u32[]{:S(2)}, u32[]{:S(2)}) collective-permute-start(bf16[4,7168]{1,0:T(4,128)(2,1)S(1)} %collective-permute-done.7.refs_8_), channel_id=1, source_target_pairs={{0,4},{1,5},{2,6},{3,7},{4,0},{5,1},{6,2},{7,3},{8,12},{9,13},{10,... | collective-permute-start | bytes 172040 | tf_op jit(solution)/shard_map/ppermute | solution.py:62
  10.7 6.9 %copy-start.4 = (bf16[4,7168]{1,0:T(4,128)(2,1)}, bf16[4,7168]{1,0:T(4,128)(2,1)S(1)}, u32[]{:S(2)}) copy-start(bf16[4,7168]{1,0:T(4,128)(2,1)S(1)} %collective-permute-done.3.refs_4_) | copy-start | bytes 172036
  10.7 5.1 %collective-permute-start.13 = (bf16[4,7168]{1,0:T(4,128)(2,1)S(1)}, bf16[4,7168]{1,0:T(4,128)(2,1)S(1)}, u32[]{:S(2)}, u32[]{:S(2)}) collective-permute-start(bf16[4,7168]{1,0:T(4,128)(2,1)S(1)} %collective-permute-done.7.refs_8_), channel_id=1, source_target_pairs={{0,6},{1,7},{2,4},{3,5},{4,2},{5,3},{6,0},{7,1},{8,14},{9,15},{10,... | collective-permute-start | bytes 172040 | tf_op jit(solution)/shard_map/ppermute | solution.py:62
  13.0 4.6 %copy-start.5 = (bf16[4,7168]{1,0:T(4,128)(2,1)}, bf16[4,7168]{1,0:T(4,128)(2,1)S(1)}, u32[]{:S(2)}) copy-start(bf16[4,7168]{1,0:T(4,128)(2,1)S(1)} %collective-permute-done.5.refs_6_) | copy-start | bytes 172036
  13.0 2.8 %collective-permute-start.8 = (bf16[4,7168]{1,0:T(4,128)(2,1)S(1)}, bf16[4,7168]{1,0:T(4,128)(2,1)S(1)}, u32[]{:S(2)}, u32[]{:S(2)}) collective-permute-start(bf16[4,7168]{1,0:T(4,128)(2,1)S(1)} %collective-permute-done.7.refs_8_), channel_id=1, source_target_pairs={{0,1},{1,0},{2,3},{3,2},{4,5},{5,4},{6,7},{7,6},{8,9},{9,8},{10,11... | collective-permute-start | bytes 172040 | tf_op jit(solution)/shard_map/ppermute | solution.py:62
  13.0 4.6 %copy-start.6 = (bf16[4,7168]{1,0:T(4,128)(2,1)}, bf16[4,7168]{1,0:T(4,128)(2,1)S(1)}, u32[]{:S(2)}) copy-start(bf16[4,7168]{1,0:T(4,128)(2,1)S(1)} %collective-permute-done.refs_1_) | copy-start | bytes 172036
  13.0 3.3 %collective-permute-start.2 = (bf16[4,7168]{1,0:T(4,128)(2,1)S(1)}, bf16[4,7168]{1,0:T(4,128)(2,1)S(1)}, u32[]{:S(2)}, u32[]{:S(2)}) collective-permute-start(bf16[4,7168]{1,0:T(4,128)(2,1)S(1)} %collective-permute-done.1.refs_2_), channel_id=1, source_target_pairs={{0,1},{1,0},{2,3},{3,2},{4,5},{5,4},{6,7},{7,6},{8,9},{9,8},{10,11... | collective-permute-start | bytes 172040 | tf_op jit(solution)/shard_map/ppermute | solution.py:62
  13.5 4.1 %copy-start.7 = (bf16[4,7168]{1,0:T(4,128)(2,1)}, bf16[4,7168]{1,0:T(4,128)(2,1)S(1)}, u32[]{:S(2)}) copy-start(bf16[4,7168]{1,0:T(4,128)(2,1)S(1)} %collective-permute-done.9.refs_10_) | copy-start | bytes 172036
  13.5 2.9 %collective-permute-start.4 = (bf16[4,7168]{1,0:T(4,128)(2,1)S(1)}, bf16[4,7168]{1,0:T(4,128)(2,1)S(1)}, u32[]{:S(2)}, u32[]{:S(2)}) collective-permute-start(bf16[4,7168]{1,0:T(4,128)(2,1)S(1)} %collective-permute-done.3.refs_4_), channel_id=1, source_target_pairs={{0,1},{1,0},{2,3},{3,2},{4,5},{5,4},{6,7},{7,6},{8,9},{9,8},{10,11... | collective-permute-start | bytes 172040 | tf_op jit(solution)/shard_map/ppermute | solution.py:62
  13.6 4.0 %copy-start.8 = (bf16[4,7168]{1,0:T(4,128)(2,1)}, bf16[4,7168]{1,0:T(4,128)(2,1)S(1)}, u32[]{:S(2)}) copy-start(bf16[4,7168]{1,0:T(4,128)(2,1)S(1)} %collective-permute-done.11.refs_12_) | copy-start | bytes 172036
  13.6 2.8 %collective-permute-start.6 = (bf16[4,7168]{1,0:T(4,128)(2,1)S(1)}, bf16[4,7168]{1,0:T(4,128)(2,1)S(1)}, u32[]{:S(2)}, u32[]{:S(2)}) collective-permute-start(bf16[4,7168]{1,0:T(4,128)(2,1)S(1)} %collective-permute-done.5.refs_6_), channel_id=1, source_target_pairs={{0,1},{1,0},{2,3},{3,2},{4,5},{5,4},{6,7},{7,6},{8,9},{9,8},{10,11... | collective-permute-start | bytes 172040 | tf_op jit(solution)/shard_map/ppermute | solution.py:62
  15.8 1.8 %copy-start.9 = (bf16[4,7168]{1,0:T(4,128)(2,1)}, bf16[4,7168]{1,0:T(4,128)(2,1)S(1)}, u32[]{:S(2)}) copy-start(bf16[4,7168]{1,0:T(4,128)(2,1)S(1)} %collective-permute-done.13.refs_14_) | copy-start | bytes 172036
  15.8 1.2 %collective-permute-start.10 = (bf16[4,7168]{1,0:T(4,128)(2,1)S(1)}, bf16[4,7168]{1,0:T(4,128)(2,1)S(1)}, u32[]{:S(2)}, u32[]{:S(2)}) collective-permute-start(bf16[4,7168]{1,0:T(4,128)(2,1)S(1)} %collective-permute-done.9.refs_10_), channel_id=1, source_target_pairs={{0,1},{1,0},{2,3},{3,2},{4,5},{5,4},{6,7},{7,6},{8,9},{9,8},{10,11... | collective-permute-start | bytes 172040 | tf_op jit(solution)/shard_map/ppermute | solution.py:62
  15.8 1.8 %copy-start.10 = (bf16[4,7168]{1,0:T(4,128)(2,1)}, bf16[4,7168]{1,0:T(4,128)(2,1)S(1)}, u32[]{:S(2)}) copy-start(bf16[4,7168]{1,0:T(4,128)(2,1)S(1)} %collective-permute-done.8.refs_9_) | copy-start | bytes 172036
  15.8 1.4 %collective-permute-start.12 = (bf16[4,7168]{1,0:T(4,128)(2,1)S(1)}, bf16[4,7168]{1,0:T(4,128)(2,1)S(1)}, u32[]{:S(2)}, u32[]{:S(2)}) collective-permute-start(bf16[4,7168]{1,0:T(4,128)(2,1)S(1)} %collective-permute-done.11.refs_12_), channel_id=1, source_target_pairs={{0,1},{1,0},{2,3},{3,2},{4,5},{5,4},{6,7},{7,6},{8,9},{9,8},{10,11... | collective-permute-start | bytes 172040 | tf_op jit(solution)/shard_map/ppermute | solution.py:62
  16.3 1.3 %copy-start.11 = (bf16[4,7168]{1,0:T(4,128)(2,1)}, bf16[4,7168]{1,0:T(4,128)(2,1)S(1)}, u32[]{:S(2)}) copy-start(bf16[4,7168]{1,0:T(4,128)(2,1)S(1)} %collective-permute-done.2.refs_3_) | copy-start | bytes 172036
  16.3 1.2 %collective-permute-start.14 = (bf16[4,7168]{1,0:T(4,128)(2,1)S(1)}, bf16[4,7168]{1,0:T(4,128)(2,1)S(1)}, u32[]{:S(2)}, u32[]{:S(2)}) collective-permute-start(bf16[4,7168]{1,0:T(4,128)(2,1)S(1)} %collective-permute-done.13.refs_14_), channel_id=1, source_target_pairs={{0,1},{1,0},{2,3},{3,2},{4,5},{5,4},{6,7},{7,6},{8,9},{9,8},{10,11... | collective-permute-start | bytes 172040 | tf_op jit(solution)/shard_map/ppermute | solution.py:62
  16.4 1.2 %copy-start.12 = (bf16[4,7168]{1,0:T(4,128)(2,1)}, bf16[4,7168]{1,0:T(4,128)(2,1)S(1)}, u32[]{:S(2)}) copy-start(bf16[4,7168]{1,0:T(4,128)(2,1)S(1)} %collective-permute-done.4.refs_5_) | copy-start | bytes 172036
  16.4 1.2 %copy-start.13 = (bf16[4,7168]{1,0:T(4,128)(2,1)}, bf16[4,7168]{1,0:T(4,128)(2,1)S(1)}, u32[]{:S(2)}) copy-start(bf16[4,7168]{1,0:T(4,128)(2,1)S(1)} %collective-permute-done.6.refs_7_) | copy-start | bytes 172036
  17.0 0.6 %copy-start.14 = (bf16[4,7168]{1,0:T(4,128)(2,1)}, bf16[4,7168]{1,0:T(4,128)(2,1)S(1)}, u32[]{:S(2)}) copy-start(bf16[4,7168]{1,0:T(4,128)(2,1)S(1)} %collective-permute-done.10.refs_11_) | copy-start | bytes 172036
  17.2 0.6 %copy-start.15 = (bf16[4,7168]{1,0:T(4,128)(2,1)}, bf16[4,7168]{1,0:T(4,128)(2,1)S(1)}, u32[]{:S(2)}) copy-start(bf16[4,7168]{1,0:T(4,128)(2,1)S(1)} %collective-permute-done.12.refs_13_) | copy-start | bytes 172036
  17.5 0.6 %copy-start.16 = (bf16[4,7168]{1,0:T(4,128)(2,1)}, bf16[4,7168]{1,0:T(4,128)(2,1)S(1)}, u32[]{:S(2)}) copy-start(bf16[4,7168]{1,0:T(4,128)(2,1)S(1)} %collective-permute-done.14.refs_15_) | copy-start | bytes 172036
  18.1 20.7 %copy-start.17 = (f32[4,2]{0,1:T(2,128)S(1)}, f32[4,2]{0,1:T(2,128)}, u32[]{:S(2)}) copy-start(f32[4,2]{0,1:T(2,128)} %param.10) | copy-start | bytes 100
  18.1 20.7 %copy-start.18 = (s32[4,2]{0,1:T(2,128)S(1)}, s32[4,2]{0,1:T(2,128)}, u32[]{:S(2)}) copy-start(s32[4,2]{0,1:T(2,128)} %param.9) | copy-start | bytes 100
  26.0 2.1 %collective-permute-start.15 = (bf16[8,4,7168]{2,1,0:T(4,128)(2,1)}, bf16[8,4,7168]{2,1,0:T(4,128)(2,1)S(1)}, u32[]{:S(2)}, u32[]{:S(2)}) collective-permute-start(bf16[8,4,7168]{2,1,0:T(4,128)(2,1)} %get-tuple-element.15), channel_id=1, source_target_pairs={{0,1},{1,0},{2,3},{3,2},{4,5},{5,4},{6,7},{7,6},{8,9},{9,8},{10,11... | collective-permute-start | bytes 1376264 | tf_op jit(solution)/shard_map/ppermute | solution.py:62
  28.1 1.0 %copy-start = (bf16[8,4,7168]{2,1,0:T(4,128)(2,1)S(1)}, bf16[8,4,7168]{2,1,0:T(4,128)(2,1)}, u32[]{:S(2)}) copy-start(bf16[8,4,7168]{2,1,0:T(4,128)(2,1)} %get-tuple-element.14.keep) | copy-start | bytes 1376260
  29.3 5.2 %collective-permute-start.19 = (bf16[4,7168]{1,0:T(4,128)(2,1)S(1)}, bf16[4,7168]{1,0:T(4,128)(2,1)S(1)}, u32[]{:S(2)}, u32[]{:S(2)}) collective-permute-start(bf16[4,7168]{1,0:T(4,128)(2,1)S(1)} %get-tuple-element.20), channel_id=1, source_target_pairs={{0,2},{1,3},{2,0},{3,1},{4,6},{5,7},{6,4},{7,5},{8,10},{9,11},{10,... | collective-permute-start | bytes 172040 | tf_op jit(solution)/shard_map/ppermute | solution.py:62
  30.8 5.6 %collective-permute-start.20 = (bf16[4,7168]{1,0:T(4,128)(2,1)S(1)}, bf16[4,7168]{1,0:T(4,128)(2,1)S(1)}, u32[]{:S(2)}, u32[]{:S(2)}) collective-permute-start(bf16[4,7168]{1,0:T(4,128)(2,1)S(1)} %get-tuple-element.21), channel_id=1, source_target_pairs={{0,4},{1,5},{2,6},{3,7},{4,0},{5,1},{6,2},{7,3},{8,12},{9,13},{10,... | collective-permute-start | bytes 172040 | tf_op jit(solution)/shard_map/ppermute | solution.py:62
  30.9 5.5 %collective-permute-start.21 = (bf16[4,7168]{1,0:T(4,128)(2,1)S(1)}, bf16[4,7168]{1,0:T(4,128)(2,1)S(1)}, u32[]{:S(2)}, u32[]{:S(2)}) collective-permute-start(bf16[4,7168]{1,0:T(4,128)(2,1)S(1)} %get-tuple-element.22), channel_id=1, source_target_pairs={{0,6},{1,7},{2,4},{3,5},{4,2},{5,3},{6,0},{7,1},{8,14},{9,15},{10,... | collective-permute-start | bytes 172040 | tf_op jit(solution)/shard_map/ppermute | solution.py:62
  32.9 6.1 %collective-permute-start.16 = (bf16[4,7168]{1,0:T(4,128)(2,1)S(1)}, bf16[4,7168]{1,0:T(4,128)(2,1)S(1)}, u32[]{:S(2)}, u32[]{:S(2)}) collective-permute-start(bf16[4,7168]{1,0:T(4,128)(2,1)S(1)} %get-tuple-element.16), channel_id=1, source_target_pairs={{0,2},{1,3},{2,0},{3,1},{4,6},{5,7},{6,4},{7,5},{8,10},{9,11},{10,... | collective-permute-start | bytes 172040 | tf_op jit(solution)/shard_map/ppermute | solution.py:62
  34.3 4.7 %collective-permute-start.17 = (bf16[4,7168]{1,0:T(4,128)(2,1)S(1)}, bf16[4,7168]{1,0:T(4,128)(2,1)S(1)}, u32[]{:S(2)}, u32[]{:S(2)}) collective-permute-start(bf16[4,7168]{1,0:T(4,128)(2,1)S(1)} %get-tuple-element.17), channel_id=1, source_target_pairs={{0,4},{1,5},{2,6},{3,7},{4,0},{5,1},{6,2},{7,3},{8,12},{9,13},{10,... | collective-permute-start | bytes 172040 | tf_op jit(solution)/shard_map/ppermute | solution.py:62
  34.5 5.4 %collective-permute-start.18 = (bf16[4,7168]{1,0:T(4,128)(2,1)S(1)}, bf16[4,7168]{1,0:T(4,128)(2,1)S(1)}, u32[]{:S(2)}, u32[]{:S(2)}) collective-permute-start(bf16[4,7168]{1,0:T(4,128)(2,1)S(1)} %get-tuple-element.18), channel_id=1, source_target_pairs={{0,6},{1,7},{2,4},{3,5},{4,2},{5,3},{6,0},{7,1},{8,14},{9,15},{10,... | collective-permute-start | bytes 172040 | tf_op jit(solution)/shard_map/ppermute | solution.py:62
  36.4 5.1 %collective-permute-start.22 = (bf16[4,7168]{1,0:T(4,128)(2,1)S(1)}, bf16[4,7168]{1,0:T(4,128)(2,1)S(1)}, u32[]{:S(2)}, u32[]{:S(2)}) collective-permute-start(bf16[4,7168]{1,0:T(4,128)(2,1)S(1)} %shard_map.75), channel_id=1, source_target_pairs={{0,8},{1,9},{2,10},{3,11},{4,12},{5,13},{6,14},{7,15},{8,0},{9,1},... | collective-permute-start | bytes 172040 | tf_op jit(solution)/shard_map/ppermute | solution.py:62
  41.6 1.0 %copy-start.1 = (bf16[8,4,7168]{2,1,0:T(4,128)(2,1)S(1)}, bf16[8,4,7168]{2,1,0:T(4,128)(2,1)}, u32[]{:S(2)}) copy-start(bf16[8,4,7168]{2,1,0:T(4,128)(2,1)} %get-tuple-element.14.keep) | copy-start | bytes 1376260

commit v2 on v0

--- a/solution.py
+++ b/solution.py
@@ -1,9 +1,17 @@
+import functools
+
 import jax
 import jax.numpy as jnp
 from jax import lax
+from jax.experimental import pallas as pl
+from jax.experimental.pallas import tpu as pltpu
 from jax.sharding import PartitionSpec as P
 
 SHARDS = 8
+CHUNKS = 4
+VMEM = pl.BlockSpec(memory_space=pltpu.VMEM)
+HBM = pl.BlockSpec(memory_space=pltpu.HBM)
+SMALL = pltpu.CompilerParams(vmem_limit_bytes=4 * 1024 * 1024)
 
 
 def slot_select(member, slots):
@@ -13,7 +21,7 @@
     )
 
 
-def body(hidden_rows, norm_gain, expert_ids, route_weights, gate_weight, up_weight, down_weight):
+def routed_body(hidden_rows, norm_gain, expert_ids, route_weights, gate_weight, up_weight, down_weight):
     devices = lax.axis_size("expert")
     experts = devices // SHARDS
     tok_rows = hidden_rows.shape[0]
@@ -49,6 +57,160 @@
     return mixed.astype(jnp.bfloat16)
 
 
+def swap(array, mask):
+    devices = lax.axis_size("expert")
+    return lax.ppermute(array, "expert", [(i, i ^ mask) for i in range(devices)])
+
+
+def rows_normed(piece, gain):
+    values = piece[...].astype(jnp.float32)
+    scale = lax.rsqrt(jnp.mean(values * values, axis=-1, keepdims=True) + 1e-06)
+    return (values * scale * gain[...]).astype(jnp.bfloat16)
+
+
+def fetch_kernel(count, *refs):
+    sources, targets, sems = refs[1 : count + 1], refs[count + 1 : -1], refs[-1]
+    copies = [pltpu.make_async_copy(s, t, sems.at[i]) for i, (s, t) in enumerate(zip(sources, targets))]
+    for copy in copies:
+        copy.start()
+    for copy in copies:
+        copy.wait()
+
+
+def in_hbm(array):
+    return pltpu.with_memory_space_constraint(array, pltpu.HBM)
+
+
+def fetch_call(after, *arrays):
+    count = len(arrays)
+    read = sum(a.size * a.dtype.itemsize for a in arrays)
+    return pl.pallas_call(
+        functools.partial(fetch_kernel, count),
+        out_shape=tuple(pltpu.VMEM(a.shape, a.dtype) for a in arrays),
+        in_specs=[VMEM] + [HBM] * count,
+        out_specs=(VMEM,) * count,
+        scratch_shapes=[pltpu.SemaphoreType.DMA((count,))],
+        compiler_params=SMALL,
+        cost_estimate=pl.CostEstimate(flops=0, bytes_accessed=2 * read, transcendentals=0),
+    )(after, *[in_hbm(a) for a in arrays])
+
+
+def norm_kernel(gain, *refs):
+    normed = refs[-1]
+    tok = refs[0].shape[0]
+    for k, piece in enumerate(refs[:-1]):
+        normed[tok * k : tok * (k + 1), :] = rows_normed(piece, gain)
+
+
+def norm_call(gain, pieces):
+    tok, width = pieces[0].shape
+    return pl.pallas_call(
+        norm_kernel,
+        out_shape=jax.ShapeDtypeStruct((tok * len(pieces), width), jnp.bfloat16),
+        in_specs=[VMEM] * (len(pieces) + 1),
+        out_specs=VMEM,
+        compiler_params=SMALL,
+    )(gain, *pieces)
+
+
+def expert_kernel(order, tok, *refs):
+    *parts, gate_w, up_w, down_w, keep, give, normed = refs
+    row = 0
+    for part in parts:
+        normed[row : row + part.shape[0], :] = part[...]
+        row += part.shape[0]
+    gate = jnp.dot(normed[...], gate_w[0], preferred_element_type=jnp.float32)
+    upper = jnp.dot(normed[...], up_w[0], preferred_element_type=jnp.float32)
+    active = (gate / (1.0 + jnp.exp(-gate)) * upper).astype(jnp.bfloat16)
+    step = down_w.shape[2] // CHUNKS
+    for c in range(CHUNKS):
+        part = slice(c * step, (c + 1) * step)
+        result = jnp.dot(active, down_w[0, :, part], preferred_element_type=jnp.float32)
+        for row, k in enumerate(order):
+            block = result[tok * row : tok * (row + 1)].astype(jnp.bfloat16)
+            if k % 2 == 0:
+                keep[k // 2, :, part] = block
+            else:
+                give[k // 2, :, part] = block
+
+
+def experts_call(order, tok, parts, weights):
+    width = parts[0].shape[1]
+    half = jax.ShapeDtypeStruct((len(order) // 2, tok, width), jnp.bfloat16)
+    return pl.pallas_call(
+        functools.partial(expert_kernel, order, tok),
+        out_shape=(half, half),
+        in_specs=[VMEM] * (len(parts) + 3),
+        out_specs=(VMEM, VMEM),
+        scratch_shapes=[pltpu.VMEM((tok * len(order), width), jnp.bfloat16)],
+        compiler_params=pltpu.CompilerParams(vmem_limit_bytes=16 * 1024 * 1024),
+    )(*parts, *weights)
+
+
+def add(a, b):
+    return a.astype(jnp.float32) + b.astype(jnp.float32)
+
+
+def pair_kernel(keep, got, *outs):
+    for i, out in enumerate(outs):
+        out[...] = add(keep[i + 1], got[i + 1]).astype(jnp.bfloat16)
+
+
+def across_kernel(own, a, b, c, total):
+    total[...] = (add(own[...], a[...]) + add(b[...], c[...])).astype(jnp.bfloat16)
+
+
+def last_kernel(tables, keep, got, a, b, c, cross, out):
+    own = add(keep[0], got[0]) + (add(a[...], b[...]) + c[...].astype(jnp.float32))
+    weight = tables[...]
+    out[...] = (weight[:, 0:1] * own + weight[:, 1:2] * cross[...].astype(jnp.float32)).astype(jnp.bfloat16)
+
+
+def small_call(kernel, outs, block, *operands):
+    shape = (block,) * outs if outs > 1 else block
+    specs = (VMEM,) * outs if outs > 1 else VMEM
+    return pl.pallas_call(
+        kernel, out_shape=shape, in_specs=[VMEM] * len(operands), out_specs=specs, compiler_params=SMALL
+    )(*operands)
+
+
+def dense_body(hidden_rows, norm_gain, expert_ids, route_weights, gate_weight, up_weight, down_weight):
+    own_expert = lax.axis_index("expert") // SHARDS
+    ids = jnp.stack([own_expert, 1 - own_expert]).astype(jnp.int32)
+    table = jnp.sum(
+        jnp.where(expert_ids[:, :, None] == ids[None, None, :], route_weights[:, :, None], 0.0), axis=1
+    )
+    x = hidden_rows
+    gain = norm_gain[None, :]
+    piece = {0: x}
+    piece[8] = swap(x, 8)
+    for k in (2, 4, 6):
+        piece[k] = swap(x, k)
+    for k in (2, 4, 6):
+        piece[8 + k] = swap(piece[8], k)
+    own = tuple(range(0, 16, 2))
+    gate_w, up_w, gain, piece[0] = fetch_call(piece[8], gate_weight, up_weight, gain, x)
+    rows = norm_call(gain, [piece[k] for k in own])
+    (down_w,) = fetch_call(rows, down_weight)
+    order = [k + c for c in (0, 1) for k in own]
+    keep, give = experts_call(order, x.shape[0], (rows, swap(rows, 1)), (gate_w, up_w, down_w))
+    got = swap(give, 1)
+    block = jax.ShapeDtypeStruct(x.shape, jnp.bfloat16)
+    sums = small_call(pair_kernel, 7, block, keep, got)
+    far = [swap(sums[3 + i], 2 * i) for i in (1, 2, 3)]
+    cross = swap(small_call(across_kernel, 1, block, sums[3], *far), 8)
+    near = [swap(sums[i - 1], 2 * i) for i in (1, 2, 3)]
+    return small_call(last_kernel, 1, block, table, keep, got, *near, cross)
+
+
+def body(*args):
+    devices = lax.axis_size("expert")
+    experts = devices // SHARDS
+    if experts == 2 and args[2].shape[1] == 2:
+        return dense_body(*args)
+    return routed_body(*args)
+
+
 def solution(mesh):
     return jax.shard_map(
         body,

time: 70.6 us -> 36.8 us (0.52); the launches traced: 69.6 us -> 36.7 us
  blocking collectives: 29.7 us -> 0 us
  starting transfers between devices: 4.48 us -> 21.8 us
  waiting for transfers between devices: 20.6 us -> 5.73 us
  matrix products: 10.4 us -> 0 us
  Pallas kernels: 0 us -> 8.76 us
  local copies, waits for them, and re-layouts: 2.23 us -> 0.11 us
  other arithmetic: 2.16 us -> 0.15 us
    all_to_all x1 -> x0, blocking collectives: 29.7 us -> none  [body(): lax.all_to_all(outgoing, 'expert', split_axis=0, concat_axis=0, tiled=True)]
    ppermute x0 -> x16, starting transfers between devices: none -> 21.8 us  [swap(): lax.ppermute(array, 'expert', [(i, i ^ mask) for i in range(devices)])]
    all_to_all x1 -> x0, waiting for transfers between devices: 20.6 us -> none  [body(): lax.all_to_all(part, 'expert', split_axis=0, concat_axis=0, tiled=True)]
    dot_general x4 -> x0, matrix products: 10.4 us -> none  [the longest x1 5.45 us: body(): jnp.dot(active, down_piece, preferred_element_type=jnp.float32)]
    pallas_call x0 -> x7, Pallas kernels: none -> 8.76 us  [the longest x2 5.24 us: fetch_call(): pl.pallas_call(functools.partial(fetch_kernel, count), out_shape=tuple((p...]
    ppermute x0 -> x16, waiting for transfers between devices: none -> 5.73 us  [swap(): lax.ppermute(array, 'expert', [(i, i ^ mask) for i in range(devices)])]
    all_to_all x1 -> x0, starting transfers between devices: 4.48 us -> none  [body(): lax.all_to_all(part, 'expert', split_axis=0, concat_axis=0, tiled=True)]
    reshape x2 -> x0, local copies, waits for them, and re-layouts: 1.46 us -> none  [the longest x1 1.26 us: body(): part = part.reshape(devices, items, width)]
  transfers between devices with their start and end apart: 1 -> 16, of which waited for: 1 -> 4; matrix products, arithmetic and copies ran while one was open for 0% -> 1% of each run, Pallas kernels for 0% -> 14%
where the time goes in v2:
time: 36.8 us; the launch traced here: 36.7 us
  starting transfers between devices  21.8 us (59%)
  Pallas kernels  8.76 us (24%)
  waiting for transfers between devices  5.73 us (16%)
    ppermute x16, starting transfers between devices, swap(): lax.ppermute(array, 'expert', [(i, i ^ mask) for i in range(devices)])  21.8 us
    ppermute x16, waiting for transfers between devices, swap(): lax.ppermute(array, 'expert', [(i, i ^ mask) for i in range(devices)])  5.73 us
    pallas_call x2, Pallas kernels, fetch_call(): pl.pallas_call(functools.partial(fetch_kernel, count), out_shape=tuple((p...  5.24 us
    pallas_call x1, Pallas kernels, experts_call(): pl.pallas_call(functools.partial(expert_kernel, order, tok), out_shape=(h...  2.11 us
    pallas_call x3, Pallas kernels, small_call(): pl.pallas_call(kernel, out_shape=shape, in_specs=[VMEM] * len(operands),...  0.96 us
  transfers between devices with their start and end apart: 16, of which 4 were waited for; matrix products, arithmetic and copies ran while one was open for 1% of the time, Pallas kernels for 14%

profile of v2, /device:TPU:0, one launch (start us, length us, event | category | flops | bytes accessed | tf_op | source)
XLA Modules:
  0.0 36.7 jit_solution(8744409469544640728)
XLA Ops:
  0.0 4.0 %collective-permute-start = (bf16[4,7168]{1,0:T(4,128)(2,1)}, bf16[4,7168]{1,0:T(4,128)(2,1)S(1)}, u32[]{:S(2)}, u32[]{:S(2)}) collective-permute-start(bf16[4,7168]{1,0:T(4,128)(2,1)} %refs_4_.1), channel_id=1, source_target_pairs={{0,8},{1,9},{2,10},{3,11},{4,12},{5,13},{6,14},{7,15},{8,0},{9,1},... | collective-permute-start | bytes 172040 | tf_op jit(solution)/shard_map/ppermute | solution.py:62
  4.0 1.5 %collective-permute-start.1 = (bf16[4,7168]{1,0:T(4,128)(2,1)}, bf16[4,7168]{1,0:T(4,128)(2,1)S(1)}, u32[]{:S(2)}, u32[]{:S(2)}) collective-permute-start(bf16[4,7168]{1,0:T(4,128)(2,1)} %refs_4_.1), channel_id=1, source_target_pairs={{0,2},{1,3},{2,0},{3,1},{4,6},{5,7},{6,4},{7,5},{8,10},{9,11},{10,... | collective-permute-start | bytes 172040 | tf_op jit(solution)/shard_map/ppermute | solution.py:62
  5.5 1.6 %collective-permute-start.2 = (bf16[4,7168]{1,0:T(4,128)(2,1)}, bf16[4,7168]{1,0:T(4,128)(2,1)S(1)}, u32[]{:S(2)}, u32[]{:S(2)}) collective-permute-start(bf16[4,7168]{1,0:T(4,128)(2,1)} %refs_4_.1), channel_id=1, source_target_pairs={{0,4},{1,5},{2,6},{3,7},{4,0},{5,1},{6,2},{7,3},{8,12},{9,13},{10,... | collective-permute-start | bytes 172040 | tf_op jit(solution)/shard_map/ppermute | solution.py:62
  7.1 0.4 %collective-permute-start.3 = (bf16[4,7168]{1,0:T(4,128)(2,1)}, bf16[4,7168]{1,0:T(4,128)(2,1)S(1)}, u32[]{:S(2)}, u32[]{:S(2)}) collective-permute-start(bf16[4,7168]{1,0:T(4,128)(2,1)} %refs_4_.1), channel_id=1, source_target_pairs={{0,6},{1,7},{2,4},{3,5},{4,2},{5,3},{6,0},{7,1},{8,14},{9,15},{10,... | collective-permute-start | bytes 172040 | tf_op jit(solution)/shard_map/ppermute | solution.py:62
  7.5 0.0 collective-permute-done.refs_0_.refs_4_
  7.5 1.5 %collective-permute-start.4 = (bf16[4,7168]{1,0:T(4,128)(2,1)S(1)}, bf16[4,7168]{1,0:T(4,128)(2,1)S(1)}, u32[]{:S(2)}, u32[]{:S(2)}) collective-permute-start(bf16[4,7168]{1,0:T(4,128)(2,1)S(1)} %collective-permute-done.refs_0_.refs_4_), channel_id=1, source_target_pairs={{0,2},{1,3},{2,0},{3,1},{4,6},{5,7},{6,4},{7,5},{8,10},{9,11},{10,... | collective-permute-start | bytes 172040 | tf_op jit(solution)/shard_map/ppermute | solution.py:62
  9.0 1.6 %collective-permute-start.5 = (bf16[4,7168]{1,0:T(4,128)(2,1)S(1)}, bf16[4,7168]{1,0:T(4,128)(2,1)S(1)}, u32[]{:S(2)}, u32[]{:S(2)}) collective-permute-start(bf16[4,7168]{1,0:T(4,128)(2,1)S(1)} %collective-permute-done.refs_0_.refs_4_), channel_id=1, source_target_pairs={{0,4},{1,5},{2,6},{3,7},{4,0},{5,1},{6,2},{7,3},{8,12},{9,13},{10,... | collective-permute-start | bytes 172040 | tf_op jit(solution)/shard_map/ppermute | solution.py:62
  10.6 0.0 collective-permute-done.1.refs_1_
  10.6 1.1 %collective-permute-start.6 = (bf16[4,7168]{1,0:T(4,128)(2,1)S(1)}, bf16[4,7168]{1,0:T(4,128)(2,1)S(1)}, u32[]{:S(2)}, u32[]{:S(2)}) collective-permute-start(bf16[4,7168]{1,0:T(4,128)(2,1)S(1)} %collective-permute-done.refs_0_.refs_4_), channel_id=1, source_target_pairs={{0,6},{1,7},{2,4},{3,5},{4,2},{5,3},{6,0},{7,1},{8,14},{9,15},{10,... | collective-permute-start | bytes 172040 | tf_op jit(solution)/shard_map/ppermute | solution.py:62
  11.7 3.2 %shard_map.73 = (bf16[1,7168,256]{2,1,0:T(8,128)(2,1)S(1)}, bf16[1,7168,256]{2,1,0:T(8,128)(2,1)S(1)}, f32[1,7168]{1,0:T(1,128)S(1)}, bf16[4,7168]{1,0:T(4,128)(2,1)S(1)}) custom-call(bf16[4,7168]{1,0:T(4,128)(2,1)S(1)} %collective-permute-done.refs_0_.refs_4_, bf16[1,7168,256]{2,1,0:T(8,128)(2,1)} %refs_1_.2, bf16[1,7168,256]{2,1,0:T(8,128)(2,1)} %refs_2_.1, ...), custom_call_target="tpu_custom_call" | custom-call | bytes 14852096 | tf_op jit(solution)/shard_map/pallas_call | solution.py:87
  14.9 0.0 collective-permute-done.2.refs_2_
  14.9 0.0 collective-permute-done.3.refs_3_
  14.9 0.0 collective-permute-done.4.refs_5_
  14.9 0.0 collective-permute-done.5.refs_6_
  14.9 0.8 %collective-permute-done.6.refs_7_ = bf16[4,7168]{1,0:T(4,128)(2,1)S(1)} collective-permute-done((bf16[4,7168]{1,0:T(4,128)(2,1)S(1)}, bf16[4,7168]{1,0:T(4,128)(2,1)S(1)}, u32[]{:S(2)}, u32[]{:S(2)}) %collective-permute-start.6) | collective-permute-done | bytes 57376 | tf_op jit(solution)/shard_map/ppermute | solution.py:62
  15.7 0.4 %shard_map.74.refs_0_ = bf16[32,7168]{1,0:T(8,128)(2,1)S(1)} custom-call(f32[1,7168]{1,0:T(1,128)S(1)} %get-tuple-element.18.gain, bf16[4,7168]{1,0:T(4,128)(2,1)S(1)} %get-tuple-element.19.refs_0_, bf16[4,7168]{1,0:T(4,128)(2,1)S(1)} %collective-permute-done.1.refs_1_, bf16[4,7168]{1,0:T(4,128)(2,1)S(1)} %collective-permute-done.2.refs_2_, ...), custom_call_target="tpu_custom_call" | custom-call | tf_op jit(solution)/shard_map/pallas_call | solution.py:107
  16.1 0.1 collective-permute-start.7
  16.2 2.0 %shard_map.75.refs_4_ = bf16[1,256,7168]{2,1,0:T(8,128)(2,1)S(1)} custom-call(bf16[32,7168]{1,0:T(8,128)(2,1)S(1)} %shard_map.74.refs_0_, bf16[1,256,7168]{2,1,0:T(8,128)(2,1)} %refs_1_.3), custom_call_target="tpu_custom_call" | custom-call | bytes 7340032 | tf_op jit(solution)/shard_map/pallas_call | solution.py:87
  18.3 0.0 collective-permute-done.7.refs_1_
  18.3 0.0 copy-start
  18.3 0.0 copy-start.1
  18.3 2.1 %shard_map.76 = (bf16[8,4,7168]{2,1,0:T(4,128)(2,1)S(1)}, bf16[8,4,7168]{2,1,0:T(4,128)(2,1)S(1)}) custom-call(bf16[32,7168]{1,0:T(8,128)(2,1)S(1)} %shard_map.74.refs_0_, bf16[32,7168]{1,0:T(8,128)(2,1)S(1)} %collective-permute-done.7.refs_1_, bf16[1,7168,256]{2,1,0:T(8,128)(2,1)S(1)} %get-tuple-element.20.refs_2_, ...), custom_call_target="tpu_custom_call" | custom-call | tf_op jit(solution)/shard_map/pallas_call | solution.py:140
  20.4 0.6 %collective-permute-start.8 = (bf16[8,4,7168]{2,1,0:T(4,128)(2,1)S(1)}, bf16[8,4,7168]{2,1,0:T(4,128)(2,1)S(1)}, u32[]{:S(2)}, u32[]{:S(2)}) collective-permute-start(bf16[8,4,7168]{2,1,0:T(4,128)(2,1)S(1)} %get-tuple-element.23), channel_id=1, source_target_pairs={{0,1},{1,0},{2,3},{3,2},{4,5},{5,4},{6,7},{7,6},{8,9},{9,8},{10,11... | collective-permute-start | bytes 1376264 | tf_op jit(solution)/shard_map/ppermute | solution.py:62
  21.0 1.4 %collective-permute-done.8.got = bf16[8,4,7168]{2,1,0:T(4,128)(2,1)S(1)} collective-permute-done((bf16[8,4,7168]{2,1,0:T(4,128)(2,1)S(1)}, bf16[8,4,7168]{2,1,0:T(4,128)(2,1)S(1)}, u32[]{:S(2)}, u32[]{:S(2)}) %collective-permute-start.8) | collective-permute-done | bytes 458784 | tf_op jit(solution)/shard_map/ppermute | solution.py:62
  22.4 0.2 shard_map.77
  22.6 0.6 %collective-permute-start.12 = (bf16[4,7168]{1,0:T(4,128)(2,1)S(1)}, bf16[4,7168]{1,0:T(4,128)(2,1)S(1)}, u32[]{:S(2)}, u32[]{:S(2)}) collective-permute-start(bf16[4,7168]{1,0:T(4,128)(2,1)S(1)} %get-tuple-element.28), channel_id=1, source_target_pairs={{0,2},{1,3},{2,0},{3,1},{4,6},{5,7},{6,4},{7,5},{8,10},{9,11},{10,... | collective-permute-start | bytes 172040 | tf_op jit(solution)/shard_map/ppermute | solution.py:62
  23.2 1.1 %collective-permute-start.13 = (bf16[4,7168]{1,0:T(4,128)(2,1)S(1)}, bf16[4,7168]{1,0:T(4,128)(2,1)S(1)}, u32[]{:S(2)}, u32[]{:S(2)}) collective-permute-start(bf16[4,7168]{1,0:T(4,128)(2,1)S(1)} %get-tuple-element.29), channel_id=1, source_target_pairs={{0,4},{1,5},{2,6},{3,7},{4,0},{5,1},{6,2},{7,3},{8,12},{9,13},{10,... | collective-permute-start | bytes 172040 | tf_op jit(solution)/shard_map/ppermute | solution.py:62
  24.3 1.8 %collective-permute-start.14 = (bf16[4,7168]{1,0:T(4,128)(2,1)S(1)}, bf16[4,7168]{1,0:T(4,128)(2,1)S(1)}, u32[]{:S(2)}, u32[]{:S(2)}) collective-permute-start(bf16[4,7168]{1,0:T(4,128)(2,1)S(1)} %get-tuple-element.30), channel_id=1, source_target_pairs={{0,6},{1,7},{2,4},{3,5},{4,2},{5,3},{6,0},{7,1},{8,14},{9,15},{10,... | collective-permute-start | bytes 172040 | tf_op jit(solution)/shard_map/ppermute | solution.py:62
  26.2 0.1 pad_add_fusion
  26.2 0.4 %collective-permute-start.10 = (bf16[4,7168]{1,0:T(4,128)(2,1)S(1)}, bf16[4,7168]{1,0:T(4,128)(2,1)S(1)}, u32[]{:S(2)}, u32[]{:S(2)}) collective-permute-start(bf16[4,7168]{1,0:T(4,128)(2,1)S(1)} %get-tuple-element.25), channel_id=1, source_target_pairs={{0,4},{1,5},{2,6},{3,7},{4,0},{5,1},{6,2},{7,3},{8,12},{9,13},{10,... | collective-permute-start | bytes 172040 | tf_op jit(solution)/shard_map/ppermute | solution.py:62
  26.7 1.5 %collective-permute-start.11 = (bf16[4,7168]{1,0:T(4,128)(2,1)S(1)}, bf16[4,7168]{1,0:T(4,128)(2,1)S(1)}, u32[]{:S(2)}, u32[]{:S(2)}) collective-permute-start(bf16[4,7168]{1,0:T(4,128)(2,1)S(1)} %get-tuple-element.26), channel_id=1, source_target_pairs={{0,6},{1,7},{2,4},{3,5},{4,2},{5,3},{6,0},{7,1},{8,14},{9,15},{10,... | collective-permute-start | bytes 172040 | tf_op jit(solution)/shard_map/ppermute | solution.py:62
  28.2 0.0 collective-permute-done.12.a
  28.2 1.5 %collective-permute-start.9 = (bf16[4,7168]{1,0:T(4,128)(2,1)S(1)}, bf16[4,7168]{1,0:T(4,128)(2,1)S(1)}, u32[]{:S(2)}, u32[]{:S(2)}) collective-permute-start(bf16[4,7168]{1,0:T(4,128)(2,1)S(1)} %get-tuple-element.24), channel_id=1, source_target_pairs={{0,2},{1,3},{2,0},{3,1},{4,6},{5,7},{6,4},{7,5},{8,10},{9,11},{10,... | collective-permute-start | bytes 172040 | tf_op jit(solution)/shard_map/ppermute | solution.py:62
  29.7 0.0 collective-permute-done.13.b
  29.7 0.5 %collective-permute-done.14.c = bf16[4,7168]{1,0:T(4,128)(2,1)S(1)} collective-permute-done((bf16[4,7168]{1,0:T(4,128)(2,1)S(1)}, bf16[4,7168]{1,0:T(4,128)(2,1)S(1)}, u32[]{:S(2)}, u32[]{:S(2)}) %collective-permute-start.14) | collective-permute-done | bytes 57376 | tf_op jit(solution)/shard_map/ppermute | solution.py:62
  30.3 2.5 %collective-permute-start.15 = (bf16[4,7168]{1,0:T(4,128)(2,1)S(1)}, bf16[4,7168]{1,0:T(4,128)(2,1)S(1)}, u32[]{:S(2)}, u32[]{:S(2)}) collective-permute-start(bf16[4,7168]{1,0:T(4,128)(2,1)S(1)} %shard_map.78), channel_id=1, source_target_pairs={{0,8},{1,9},{2,10},{3,11},{4,12},{5,13},{6,14},{7,15},{8,0},{9,1},... | collective-permute-start | bytes 172040 | tf_op jit(solution)/shard_map/ppermute | solution.py:62
  32.8 0.0 copy-done
  32.8 0.0 copy-done.1
  32.8 0.1 fusion
  32.8 0.1 copy.10.tables
  32.9 0.0 collective-permute-done.10.b
  32.9 0.0 collective-permute-done.11.c
  32.9 0.0 collective-permute-done.9.a
  33.0 3.0 %collective-permute-done.15.cross = bf16[4,7168]{1,0:T(4,128)(2,1)S(1)} collective-permute-done((bf16[4,7168]{1,0:T(4,128)(2,1)S(1)}, bf16[4,7168]{1,0:T(4,128)(2,1)S(1)}, u32[]{:S(2)}, u32[]{:S(2)}) %collective-permute-start.15) | collective-permute-done | bytes 57376 | tf_op jit(solution)/shard_map/ppermute | solution.py:62
  35.9 0.7 %shard_map.79 = bf16[4,7168]{1,0:T(4,128)(2,1)} custom-call(f32[4,2]{1,0:T(4,128)S(1)} %copy.10.tables, bf16[8,4,7168]{2,1,0:T(4,128)(2,1)S(1)} %get-tuple-element.22.keep, bf16[8,4,7168]{2,1,0:T(4,128)(2,1)S(1)} %collective-permute-done.8.got, bf16[4,7168]{1,0:T(4,128)(2,1)S(1)} %collective-permute-done.9.a, bf16[4,7168]{1,0:T(4,128)(2,1)S(1)} %collective-permute-done.10.b, ...), custom_call_target="tpu_custom_call" | custom-call | tf_op jit(solution)/shard_map/pallas_call | solution.py:172
  (1 shorter events, 0.0 us)
Async XLA Ops:
  0.0 7.5 %collective-permute-start = (bf16[4,7168]{1,0:T(4,128)(2,1)}, bf16[4,7168]{1,0:T(4,128)(2,1)S(1)}, u32[]{:S(2)}, u32[]{:S(2)}) collective-permute-start(bf16[4,7168]{1,0:T(4,128)(2,1)} %refs_4_.1), channel_id=1, source_target_pairs={{0,8},{1,9},{2,10},{3,11},{4,12},{5,13},{6,14},{7,15},{8,0},{9,1},... | collective-permute-start | bytes 172040 | tf_op jit(solution)/shard_map/ppermute | solution.py:62
  4.0 6.6 %collective-permute-start.1 = (bf16[4,7168]{1,0:T(4,128)(2,1)}, bf16[4,7168]{1,0:T(4,128)(2,1)S(1)}, u32[]{:S(2)}, u32[]{:S(2)}) collective-permute-start(bf16[4,7168]{1,0:T(4,128)(2,1)} %refs_4_.1), channel_id=1, source_target_pairs={{0,2},{1,3},{2,0},{3,1},{4,6},{5,7},{6,4},{7,5},{8,10},{9,11},{10,... | collective-permute-start | bytes 172040 | tf_op jit(solution)/shard_map/ppermute | solution.py:62
  5.5 9.4 %collective-permute-start.2 = (bf16[4,7168]{1,0:T(4,128)(2,1)}, bf16[4,7168]{1,0:T(4,128)(2,1)S(1)}, u32[]{:S(2)}, u32[]{:S(2)}) collective-permute-start(bf16[4,7168]{1,0:T(4,128)(2,1)} %refs_4_.1), channel_id=1, source_target_pairs={{0,4},{1,5},{2,6},{3,7},{4,0},{5,1},{6,2},{7,3},{8,12},{9,13},{10,... | collective-permute-start | bytes 172040 | tf_op jit(solution)/shard_map/ppermute | solution.py:62
  7.1 7.8 %collective-permute-start.3 = (bf16[4,7168]{1,0:T(4,128)(2,1)}, bf16[4,7168]{1,0:T(4,128)(2,1)S(1)}, u32[]{:S(2)}, u32[]{:S(2)}) collective-permute-start(bf16[4,7168]{1,0:T(4,128)(2,1)} %refs_4_.1), channel_id=1, source_target_pairs={{0,6},{1,7},{2,4},{3,5},{4,2},{5,3},{6,0},{7,1},{8,14},{9,15},{10,... | collective-permute-start | bytes 172040 | tf_op jit(solution)/shard_map/ppermute | solution.py:62
  7.5 7.4 %collective-permute-start.4 = (bf16[4,7168]{1,0:T(4,128)(2,1)S(1)}, bf16[4,7168]{1,0:T(4,128)(2,1)S(1)}, u32[]{:S(2)}, u32[]{:S(2)}) collective-permute-start(bf16[4,7168]{1,0:T(4,128)(2,1)S(1)} %collective-permute-done.refs_0_.refs_4_), channel_id=1, source_target_pairs={{0,2},{1,3},{2,0},{3,1},{4,6},{5,7},{6,4},{7,5},{8,10},{9,11},{10,... | collective-permute-start | bytes 172040 | tf_op jit(solution)/shard_map/ppermute | solution.py:62
  9.0 5.9 %collective-permute-start.5 = (bf16[4,7168]{1,0:T(4,128)(2,1)S(1)}, bf16[4,7168]{1,0:T(4,128)(2,1)S(1)}, u32[]{:S(2)}, u32[]{:S(2)}) collective-permute-start(bf16[4,7168]{1,0:T(4,128)(2,1)S(1)} %collective-permute-done.refs_0_.refs_4_), channel_id=1, source_target_pairs={{0,4},{1,5},{2,6},{3,7},{4,0},{5,1},{6,2},{7,3},{8,12},{9,13},{10,... | collective-permute-start | bytes 172040 | tf_op jit(solution)/shard_map/ppermute | solution.py:62
  10.6 5.1 %collective-permute-start.6 = (bf16[4,7168]{1,0:T(4,128)(2,1)S(1)}, bf16[4,7168]{1,0:T(4,128)(2,1)S(1)}, u32[]{:S(2)}, u32[]{:S(2)}) collective-permute-start(bf16[4,7168]{1,0:T(4,128)(2,1)S(1)} %collective-permute-done.refs_0_.refs_4_), channel_id=1, source_target_pairs={{0,6},{1,7},{2,4},{3,5},{4,2},{5,3},{6,0},{7,1},{8,14},{9,15},{10,... | collective-permute-start | bytes 172040 | tf_op jit(solution)/shard_map/ppermute | solution.py:62
  16.1 2.1 %collective-permute-start.7 = (bf16[32,7168]{1,0:T(8,128)(2,1)S(1)}, bf16[32,7168]{1,0:T(8,128)(2,1)S(1)}, u32[]{:S(2)}, u32[]{:S(2)}) collective-permute-start(bf16[32,7168]{1,0:T(8,128)(2,1)S(1)} %shard_map.74.refs_0_), channel_id=1, source_target_pairs={{0,1},{1,0},{2,3},{3,2},{4,5},{5,4},{6,7},{7,6},{8,9},{9,8},{10,11... | collective-permute-start | bytes 1376264 | tf_op jit(solution)/shard_map/ppermute | solution.py:62
  18.3 14.5 %copy-start = (f32[4,2]{0,1:T(2,128)S(1)}, f32[4,2]{0,1:T(2,128)}, u32[]{:S(2)}) copy-start(f32[4,2]{0,1:T(2,128)} %param.10) | copy-start | bytes 100
  18.3 14.5 %copy-start.1 = (s32[4,2]{0,1:T(2,128)S(1)}, s32[4,2]{0,1:T(2,128)}, u32[]{:S(2)}) copy-start(s32[4,2]{0,1:T(2,128)} %param.9) | copy-start | bytes 100
  20.4 2.0 %collective-permute-start.8 = (bf16[8,4,7168]{2,1,0:T(4,128)(2,1)S(1)}, bf16[8,4,7168]{2,1,0:T(4,128)(2,1)S(1)}, u32[]{:S(2)}, u32[]{:S(2)}) collective-permute-start(bf16[8,4,7168]{2,1,0:T(4,128)(2,1)S(1)} %get-tuple-element.23), channel_id=1, source_target_pairs={{0,1},{1,0},{2,3},{3,2},{4,5},{5,4},{6,7},{7,6},{8,9},{9,8},{10,11... | collective-permute-start | bytes 1376264 | tf_op jit(solution)/shard_map/ppermute | solution.py:62
  22.6 5.6 %collective-permute-start.12 = (bf16[4,7168]{1,0:T(4,128)(2,1)S(1)}, bf16[4,7168]{1,0:T(4,128)(2,1)S(1)}, u32[]{:S(2)}, u32[]{:S(2)}) collective-permute-start(bf16[4,7168]{1,0:T(4,128)(2,1)S(1)} %get-tuple-element.28), channel_id=1, source_target_pairs={{0,2},{1,3},{2,0},{3,1},{4,6},{5,7},{6,4},{7,5},{8,10},{9,11},{10,... | collective-permute-start | bytes 172040 | tf_op jit(solution)/shard_map/ppermute | solution.py:62
  23.2 6.5 %collective-permute-start.13 = (bf16[4,7168]{1,0:T(4,128)(2,1)S(1)}, bf16[4,7168]{1,0:T(4,128)(2,1)S(1)}, u32[]{:S(2)}, u32[]{:S(2)}) collective-permute-start(bf16[4,7168]{1,0:T(4,128)(2,1)S(1)} %get-tuple-element.29), channel_id=1, source_target_pairs={{0,4},{1,5},{2,6},{3,7},{4,0},{5,1},{6,2},{7,3},{8,12},{9,13},{10,... | collective-permute-start | bytes 172040 | tf_op jit(solution)/shard_map/ppermute | solution.py:62
  24.3 5.9 %collective-permute-start.14 = (bf16[4,7168]{1,0:T(4,128)(2,1)S(1)}, bf16[4,7168]{1,0:T(4,128)(2,1)S(1)}, u32[]{:S(2)}, u32[]{:S(2)}) collective-permute-start(bf16[4,7168]{1,0:T(4,128)(2,1)S(1)} %get-tuple-element.30), channel_id=1, source_target_pairs={{0,6},{1,7},{2,4},{3,5},{4,2},{5,3},{6,0},{7,1},{8,14},{9,15},{10,... | collective-permute-start | bytes 172040 | tf_op jit(solution)/shard_map/ppermute | solution.py:62
  26.2 6.7 %collective-permute-start.10 = (bf16[4,7168]{1,0:T(4,128)(2,1)S(1)}, bf16[4,7168]{1,0:T(4,128)(2,1)S(1)}, u32[]{:S(2)}, u32[]{:S(2)}) collective-permute-start(bf16[4,7168]{1,0:T(4,128)(2,1)S(1)} %get-tuple-element.25), channel_id=1, source_target_pairs={{0,4},{1,5},{2,6},{3,7},{4,0},{5,1},{6,2},{7,3},{8,12},{9,13},{10,... | collective-permute-start | bytes 172040 | tf_op jit(solution)/shard_map/ppermute | solution.py:62
  26.7 6.3 %collective-permute-start.11 = (bf16[4,7168]{1,0:T(4,128)(2,1)S(1)}, bf16[4,7168]{1,0:T(4,128)(2,1)S(1)}, u32[]{:S(2)}, u32[]{:S(2)}) collective-permute-start(bf16[4,7168]{1,0:T(4,128)(2,1)S(1)} %get-tuple-element.26), channel_id=1, source_target_pairs={{0,6},{1,7},{2,4},{3,5},{4,2},{5,3},{6,0},{7,1},{8,14},{9,15},{10,... | collective-permute-start | bytes 172040 | tf_op jit(solution)/shard_map/ppermute | solution.py:62
  28.2 4.7 %collective-permute-start.9 = (bf16[4,7168]{1,0:T(4,128)(2,1)S(1)}, bf16[4,7168]{1,0:T(4,128)(2,1)S(1)}, u32[]{:S(2)}, u32[]{:S(2)}) collective-permute-start(bf16[4,7168]{1,0:T(4,128)(2,1)S(1)} %get-tuple-element.24), channel_id=1, source_target_pairs={{0,2},{1,3},{2,0},{3,1},{4,6},{5,7},{6,4},{7,5},{8,10},{9,11},{10,... | collective-permute-start | bytes 172040 | tf_op jit(solution)/shard_map/ppermute | solution.py:62
  30.3 5.6 %collective-permute-start.15 = (bf16[4,7168]{1,0:T(4,128)(2,1)S(1)}, bf16[4,7168]{1,0:T(4,128)(2,1)S(1)}, u32[]{:S(2)}, u32[]{:S(2)}) collective-permute-start(bf16[4,7168]{1,0:T(4,128)(2,1)S(1)} %shard_map.78), channel_id=1, source_target_pairs={{0,8},{1,9},{2,10},{3,11},{4,12},{5,13},{6,14},{7,15},{8,0},{9,1},... | collective-permute-start | bytes 172040 | tf_op jit(solution)/shard_map/ppermute | solution.py:62

commit v3 on v2

--- a/solution.py
+++ b/solution.py
@@ -9,6 +9,7 @@
 
 SHARDS = 8
 CHUNKS = 4
+LINKS = ((2, 4), (6,), (4, 2))
 VMEM = pl.BlockSpec(memory_space=pltpu.VMEM)
 HBM = pl.BlockSpec(memory_space=pltpu.HBM)
 SMALL = pltpu.CompilerParams(vmem_limit_bytes=4 * 1024 * 1024)
@@ -57,9 +58,9 @@
     return mixed.astype(jnp.bfloat16)
 
 
-def swap(array, mask):
+def swap(array, *masks):
     devices = lax.axis_size("expert")
-    return lax.ppermute(array, "expert", [(i, i ^ mask) for i in range(devices)])
+    return lax.ppermute(array, "expert", [(i, i ^ masks[i % len(masks)]) for i in range(devices)])
 
 
 def rows_normed(piece, gain):
@@ -113,7 +114,7 @@
     )(gain, *pieces)
 
 
-def expert_kernel(order, tok, *refs):
+def expert_kernel(*refs):
     *parts, gate_w, up_w, down_w, keep, give, normed = refs
     row = 0
     for part in parts:
@@ -126,23 +127,22 @@
     for c in range(CHUNKS):
         part = slice(c * step, (c + 1) * step)
         result = jnp.dot(active, down_w[0, :, part], preferred_element_type=jnp.float32)
-        for row, k in enumerate(order):
-            block = result[tok * row : tok * (row + 1)].astype(jnp.bfloat16)
-            if k % 2 == 0:
-                keep[k // 2, :, part] = block
-            else:
-                give[k // 2, :, part] = block
-
-
-def experts_call(order, tok, parts, weights):
-    width = parts[0].shape[1]
-    half = jax.ShapeDtypeStruct((len(order) // 2, tok, width), jnp.bfloat16)
-    return pl.pallas_call(
-        functools.partial(expert_kernel, order, tok),
+        for half, out in enumerate((keep, give)):
+            blocks, tok, _ = out.shape
+            for k in range(blocks):
+                row = (half * blocks + k) * tok
+                out[k, :, part] = result[row : row + tok].astype(jnp.bfloat16)
+
+
+def experts_call(tok, parts, weights):
+    rows, width = parts[0].shape
+    half = jax.ShapeDtypeStruct((rows // tok, tok, width), jnp.bfloat16)
+    return pl.pallas_call(
+        expert_kernel,
         out_shape=(half, half),
         in_specs=[VMEM] * (len(parts) + 3),
         out_specs=(VMEM, VMEM),
-        scratch_shapes=[pltpu.VMEM((tok * len(order), width), jnp.bfloat16)],
+        scratch_shapes=[pltpu.VMEM((2 * rows, width), jnp.bfloat16)],
         compiler_params=pltpu.CompilerParams(vmem_limit_bytes=16 * 1024 * 1024),
     )(*parts, *weights)
 
@@ -182,24 +182,19 @@
     )
     x = hidden_rows
     gain = norm_gain[None, :]
-    piece = {0: x}
-    piece[8] = swap(x, 8)
-    for k in (2, 4, 6):
-        piece[k] = swap(x, k)
-    for k in (2, 4, 6):
-        piece[8 + k] = swap(piece[8], k)
-    own = tuple(range(0, 16, 2))
-    gate_w, up_w, gain, piece[0] = fetch_call(piece[8], gate_weight, up_weight, gain, x)
-    rows = norm_call(gain, [piece[k] for k in own])
+    far_rows = swap(x, 8)
+    near_pieces = [swap(x, *masks) for masks in LINKS]
+    far_pieces = [swap(far_rows, *masks) for masks in LINKS]
+    gate_w, up_w, gain, own = fetch_call(far_rows, gate_weight, up_weight, gain, x)
+    rows = norm_call(gain, [own, far_rows, *near_pieces, *far_pieces])
     (down_w,) = fetch_call(rows, down_weight)
-    order = [k + c for c in (0, 1) for k in own]
-    keep, give = experts_call(order, x.shape[0], (rows, swap(rows, 1)), (gate_w, up_w, down_w))
+    keep, give = experts_call(x.shape[0], (rows, swap(rows, 1)), (gate_w, up_w, down_w))
     got = swap(give, 1)
     block = jax.ShapeDtypeStruct(x.shape, jnp.bfloat16)
     sums = small_call(pair_kernel, 7, block, keep, got)
-    far = [swap(sums[3 + i], 2 * i) for i in (1, 2, 3)]
-    cross = swap(small_call(across_kernel, 1, block, sums[3], *far), 8)
-    near = [swap(sums[i - 1], 2 * i) for i in (1, 2, 3)]
+    far = [swap(part, *masks) for part, masks in zip(sums[4:], LINKS)]
+    cross = swap(small_call(across_kernel, 1, block, sums[0], *far), 8)
+    near = [swap(part, *masks) for part, masks in zip(sums[1:4], LINKS)]
     return small_call(last_kernel, 1, block, table, keep, got, *near, cross)
 
 

time: 36.8 us -> 34.9 us (0.948)
  waiting for transfers between devices: 5.73 us -> 4.47 us
  starting transfers between devices: 21.8 us -> 21.1 us
    ppermute x16, waiting for transfers between devices: 5.73 us -> 4.47 us  [swap(): lax.ppermute(array, 'expert', [(i, i ^ masks[i % len(masks)]) for i in ra...]
    ppermute x16, starting transfers between devices: 21.8 us -> 21.1 us  [swap(): lax.ppermute(array, 'expert', [(i, i ^ masks[i % len(masks)]) for i in ra...]
  transfers between devices with their start and end apart: 16 -> 16, of which waited for: 4 -> 4; matrix products, arithmetic and copies ran while one was open for 1% -> 1% of each run, Pallas kernels for 14% -> 15%
where the time goes in v3:
time: 34.9 us; the launch traced here: 34.7 us
  starting transfers between devices  21.1 us (60%)
  Pallas kernels  8.76 us (25%)
  waiting for transfers between devices  4.47 us (13%)
    ppermute x16, starting transfers between devices, swap(): lax.ppermute(array, 'expert', [(i, i ^ masks[i % len(masks)]) for i in ra...  21.1 us
    pallas_call x2, Pallas kernels, fetch_call(): pl.pallas_call(functools.partial(fetch_kernel, count), out_shape=tuple((p...  5.24 us
    ppermute x16, waiting for transfers between devices, swap(): lax.ppermute(array, 'expert', [(i, i ^ masks[i % len(masks)]) for i in ra...  4.47 us
    pallas_call x1, Pallas kernels, experts_call(): pl.pallas_call(expert_kernel, out_shape=(half, half), in_specs=[VMEM] * (...  2.11 us
    pallas_call x3, Pallas kernels, small_call(): pl.pallas_call(kernel, out_shape=shape, in_specs=[VMEM] * len(operands),...  0.96 us
  transfers between devices with their start and end apart: 16, of which 4 were waited for; matrix products, arithmetic and copies ran while one was open for 1% of the time, Pallas kernels for 15%

profile of v3, /device:TPU:0, one launch (start us, length us, event | category | flops | bytes accessed | tf_op | source)
XLA Modules:
  0.0 34.7 jit_solution(13289246058661402821)
XLA Ops:
  0.0 4.0 %collective-permute-start = (bf16[4,7168]{1,0:T(4,128)(2,1)}, bf16[4,7168]{1,0:T(4,128)(2,1)S(1)}, u32[]{:S(2)}, u32[]{:S(2)}) collective-permute-start(bf16[4,7168]{1,0:T(4,128)(2,1)} %refs_4_.1), channel_id=1, source_target_pairs={{0,8},{1,9},{2,10},{3,11},{4,12},{5,13},{6,14},{7,15},{8,0},{9,1},... | collective-permute-start | bytes 172040 | tf_op jit(solution)/shard_map/ppermute | solution.py:63
  4.0 1.5 %collective-permute-start.1 = (bf16[4,7168]{1,0:T(4,128)(2,1)}, bf16[4,7168]{1,0:T(4,128)(2,1)S(1)}, u32[]{:S(2)}, u32[]{:S(2)}) collective-permute-start(bf16[4,7168]{1,0:T(4,128)(2,1)} %refs_4_.1), channel_id=1, source_target_pairs={{0,2},{1,5},{2,0},{3,7},{4,6},{5,1},{6,4},{7,3},{8,10},{9,13},{10,... | collective-permute-start | bytes 172040 | tf_op jit(solution)/shard_map/ppermute | solution.py:63
  5.5 1.5 %collective-permute-start.2 = (bf16[4,7168]{1,0:T(4,128)(2,1)}, bf16[4,7168]{1,0:T(4,128)(2,1)S(1)}, u32[]{:S(2)}, u32[]{:S(2)}) collective-permute-start(bf16[4,7168]{1,0:T(4,128)(2,1)} %refs_4_.1), channel_id=1, source_target_pairs={{0,6},{1,7},{2,4},{3,5},{4,2},{5,3},{6,0},{7,1},{8,14},{9,15},{10,... | collective-permute-start | bytes 172040 | tf_op jit(solution)/shard_map/ppermute | solution.py:63
  7.1 0.4 %collective-permute-start.3 = (bf16[4,7168]{1,0:T(4,128)(2,1)}, bf16[4,7168]{1,0:T(4,128)(2,1)S(1)}, u32[]{:S(2)}, u32[]{:S(2)}) collective-permute-start(bf16[4,7168]{1,0:T(4,128)(2,1)} %refs_4_.1), channel_id=1, source_target_pairs={{0,4},{1,3},{2,6},{3,1},{4,0},{5,7},{6,2},{7,5},{8,12},{9,11},{10,... | collective-permute-start | bytes 172040 | tf_op jit(solution)/shard_map/ppermute | solution.py:63
  7.5 0.0 collective-permute-done.refs_0_.refs_1_
  7.5 1.5 %collective-permute-start.4 = (bf16[4,7168]{1,0:T(4,128)(2,1)S(1)}, bf16[4,7168]{1,0:T(4,128)(2,1)S(1)}, u32[]{:S(2)}, u32[]{:S(2)}) collective-permute-start(bf16[4,7168]{1,0:T(4,128)(2,1)S(1)} %collective-permute-done.refs_0_.refs_1_), channel_id=1, source_target_pairs={{0,2},{1,5},{2,0},{3,7},{4,6},{5,1},{6,4},{7,3},{8,10},{9,13},{10,... | collective-permute-start | bytes 172040 | tf_op jit(solution)/shard_map/ppermute | solution.py:63
  9.0 1.5 %collective-permute-start.5 = (bf16[4,7168]{1,0:T(4,128)(2,1)S(1)}, bf16[4,7168]{1,0:T(4,128)(2,1)S(1)}, u32[]{:S(2)}, u32[]{:S(2)}) collective-permute-start(bf16[4,7168]{1,0:T(4,128)(2,1)S(1)} %collective-permute-done.refs_0_.refs_1_), channel_id=1, source_target_pairs={{0,6},{1,7},{2,4},{3,5},{4,2},{5,3},{6,0},{7,1},{8,14},{9,15},{10,... | collective-permute-start | bytes 172040 | tf_op jit(solution)/shard_map/ppermute | solution.py:63
  10.6 0.0 collective-permute-done.1.refs_2_
  10.6 0.5 %collective-permute-start.6 = (bf16[4,7168]{1,0:T(4,128)(2,1)S(1)}, bf16[4,7168]{1,0:T(4,128)(2,1)S(1)}, u32[]{:S(2)}, u32[]{:S(2)}) collective-permute-start(bf16[4,7168]{1,0:T(4,128)(2,1)S(1)} %collective-permute-done.refs_0_.refs_1_), channel_id=1, source_target_pairs={{0,4},{1,3},{2,6},{3,1},{4,0},{5,7},{6,2},{7,5},{8,12},{9,11},{10,... | collective-permute-start | bytes 172040 | tf_op jit(solution)/shard_map/ppermute | solution.py:63
  11.0 3.2 %shard_map.73 = (bf16[1,7168,256]{2,1,0:T(8,128)(2,1)S(1)}, bf16[1,7168,256]{2,1,0:T(8,128)(2,1)S(1)}, f32[1,7168]{1,0:T(1,128)S(1)}, bf16[4,7168]{1,0:T(4,128)(2,1)S(1)}) custom-call(bf16[4,7168]{1,0:T(4,128)(2,1)S(1)} %collective-permute-done.refs_0_.refs_1_, bf16[1,7168,256]{2,1,0:T(8,128)(2,1)} %refs_1_.2, bf16[1,7168,256]{2,1,0:T(8,128)(2,1)} %refs_2_.1, ...), custom_call_target="tpu_custom_call" | custom-call | bytes 14852096 | tf_op jit(solution)/shard_map/pallas_call | solution.py:88
  14.2 0.0 collective-permute-done.2.refs_3_
  14.2 0.0 collective-permute-done.3.refs_4_
  14.2 0.0 collective-permute-done.4.refs_5_
  14.3 0.0 collective-permute-done.5.refs_6_
  14.3 0.5 %collective-permute-done.6.refs_7_ = bf16[4,7168]{1,0:T(4,128)(2,1)S(1)} collective-permute-done((bf16[4,7168]{1,0:T(4,128)(2,1)S(1)}, bf16[4,7168]{1,0:T(4,128)(2,1)S(1)}, u32[]{:S(2)}, u32[]{:S(2)}) %collective-permute-start.6) | collective-permute-done | bytes 57376 | tf_op jit(solution)/shard_map/ppermute | solution.py:63
  14.8 0.4 %shard_map.74.refs_0_ = bf16[32,7168]{1,0:T(8,128)(2,1)S(1)} custom-call(f32[1,7168]{1,0:T(1,128)S(1)} %get-tuple-element.18.gain, bf16[4,7168]{1,0:T(4,128)(2,1)S(1)} %get-tuple-element.19.refs_0_, bf16[4,7168]{1,0:T(4,128)(2,1)S(1)} %collective-permute-done.refs_0_.refs_1_, bf16[4,7168]{1,0:T(4,128)(2,1)S(1)} %collective-permute-done.1.refs_2_, ...), custom_call_target="tpu_custom_call" | custom-call | tf_op jit(solution)/shard_map/pallas_call | solution.py:108
  15.2 0.1 collective-permute-start.7
  15.3 2.0 %shard_map.75.refs_4_ = bf16[1,256,7168]{2,1,0:T(8,128)(2,1)S(1)} custom-call(bf16[32,7168]{1,0:T(8,128)(2,1)S(1)} %shard_map.74.refs_0_, bf16[1,256,7168]{2,1,0:T(8,128)(2,1)} %refs_1_.3), custom_call_target="tpu_custom_call" | custom-call | bytes 7340032 | tf_op jit(solution)/shard_map/pallas_call | solution.py:88
  17.3 0.0 collective-permute-done.7.refs_1_
  17.3 0.0 copy-start
  17.4 0.0 copy-start.1
  17.4 2.1 %shard_map.76 = (bf16[8,4,7168]{2,1,0:T(4,128)(2,1)S(1)}, bf16[8,4,7168]{2,1,0:T(4,128)(2,1)S(1)}) custom-call(bf16[32,7168]{1,0:T(8,128)(2,1)S(1)} %shard_map.74.refs_0_, bf16[32,7168]{1,0:T(8,128)(2,1)S(1)} %collective-permute-done.7.refs_1_, bf16[1,7168,256]{2,1,0:T(8,128)(2,1)S(1)} %get-tuple-element.20.refs_2_, ...), custom_call_target="tpu_custom_call" | custom-call | tf_op jit(solution)/shard_map/pallas_call | solution.py:140
  19.5 0.6 %collective-permute-start.8 = (bf16[8,4,7168]{2,1,0:T(4,128)(2,1)S(1)}, bf16[8,4,7168]{2,1,0:T(4,128)(2,1)S(1)}, u32[]{:S(2)}, u32[]{:S(2)}) collective-permute-start(bf16[8,4,7168]{2,1,0:T(4,128)(2,1)S(1)} %get-tuple-element.23), channel_id=1, source_target_pairs={{0,1},{1,0},{2,3},{3,2},{4,5},{5,4},{6,7},{7,6},{8,9},{9,8},{10,11... | collective-permute-start | bytes 1376264 | tf_op jit(solution)/shard_map/ppermute | solution.py:63
  20.1 1.4 %collective-permute-done.8.got = bf16[8,4,7168]{2,1,0:T(4,128)(2,1)S(1)} collective-permute-done((bf16[8,4,7168]{2,1,0:T(4,128)(2,1)S(1)}, bf16[8,4,7168]{2,1,0:T(4,128)(2,1)S(1)}, u32[]{:S(2)}, u32[]{:S(2)}) %collective-permute-start.8) | collective-permute-done | bytes 458784 | tf_op jit(solution)/shard_map/ppermute | solution.py:63
  21.5 0.2 shard_map.77
  21.7 1.6 %collective-permute-start.12 = (bf16[4,7168]{1,0:T(4,128)(2,1)S(1)}, bf16[4,7168]{1,0:T(4,128)(2,1)S(1)}, u32[]{:S(2)}, u32[]{:S(2)}) collective-permute-start(bf16[4,7168]{1,0:T(4,128)(2,1)S(1)} %get-tuple-element.28), channel_id=1, source_target_pairs={{0,2},{1,5},{2,0},{3,7},{4,6},{5,1},{6,4},{7,3},{8,10},{9,13},{10,... | collective-permute-start | bytes 172040 | tf_op jit(solution)/shard_map/ppermute | solution.py:63
  23.2 1.1 %collective-permute-start.13 = (bf16[4,7168]{1,0:T(4,128)(2,1)S(1)}, bf16[4,7168]{1,0:T(4,128)(2,1)S(1)}, u32[]{:S(2)}, u32[]{:S(2)}) collective-permute-start(bf16[4,7168]{1,0:T(4,128)(2,1)S(1)} %get-tuple-element.29), channel_id=1, source_target_pairs={{0,6},{1,7},{2,4},{3,5},{4,2},{5,3},{6,0},{7,1},{8,14},{9,15},{10,... | collective-permute-start | bytes 172040 | tf_op jit(solution)/shard_map/ppermute | solution.py:63
  24.3 0.9 %collective-permute-start.14 = (bf16[4,7168]{1,0:T(4,128)(2,1)S(1)}, bf16[4,7168]{1,0:T(4,128)(2,1)S(1)}, u32[]{:S(2)}, u32[]{:S(2)}) collective-permute-start(bf16[4,7168]{1,0:T(4,128)(2,1)S(1)} %get-tuple-element.30), channel_id=1, source_target_pairs={{0,4},{1,3},{2,6},{3,1},{4,0},{5,7},{6,2},{7,5},{8,12},{9,11},{10,... | collective-permute-start | bytes 172040 | tf_op jit(solution)/shard_map/ppermute | solution.py:63
  25.2 0.1 pad_add_fusion
  25.3 2.0 %collective-permute-start.10 = (bf16[4,7168]{1,0:T(4,128)(2,1)S(1)}, bf16[4,7168]{1,0:T(4,128)(2,1)S(1)}, u32[]{:S(2)}, u32[]{:S(2)}) collective-permute-start(bf16[4,7168]{1,0:T(4,128)(2,1)S(1)} %get-tuple-element.25), channel_id=1, source_target_pairs={{0,6},{1,7},{2,4},{3,5},{4,2},{5,3},{6,0},{7,1},{8,14},{9,15},{10,... | collective-permute-start | bytes 172040 | tf_op jit(solution)/shard_map/ppermute | solution.py:63
  27.3 0.9 %collective-permute-start.11 = (bf16[4,7168]{1,0:T(4,128)(2,1)S(1)}, bf16[4,7168]{1,0:T(4,128)(2,1)S(1)}, u32[]{:S(2)}, u32[]{:S(2)}) collective-permute-start(bf16[4,7168]{1,0:T(4,128)(2,1)S(1)} %get-tuple-element.26), channel_id=1, source_target_pairs={{0,4},{1,3},{2,6},{3,1},{4,0},{5,7},{6,2},{7,5},{8,12},{9,11},{10,... | collective-permute-start | bytes 172040 | tf_op jit(solution)/shard_map/ppermute | solution.py:63
  28.3 0.0 collective-permute-done.12.a
  28.3 0.5 %collective-permute-start.9 = (bf16[4,7168]{1,0:T(4,128)(2,1)S(1)}, bf16[4,7168]{1,0:T(4,128)(2,1)S(1)}, u32[]{:S(2)}, u32[]{:S(2)}) collective-permute-start(bf16[4,7168]{1,0:T(4,128)(2,1)S(1)} %get-tuple-element.24), channel_id=1, source_target_pairs={{0,2},{1,5},{2,0},{3,7},{4,6},{5,1},{6,4},{7,3},{8,10},{9,13},{10,... | collective-permute-start | bytes 172040 | tf_op jit(solution)/shard_map/ppermute | solution.py:63
  28.8 0.0 collective-permute-done.13.b
  28.8 0.0 collective-permute-done.14.c
  28.9 2.5 %collective-permute-start.15 = (bf16[4,7168]{1,0:T(4,128)(2,1)S(1)}, bf16[4,7168]{1,0:T(4,128)(2,1)S(1)}, u32[]{:S(2)}, u32[]{:S(2)}) collective-permute-start(bf16[4,7168]{1,0:T(4,128)(2,1)S(1)} %shard_map.78), channel_id=1, source_target_pairs={{0,8},{1,9},{2,10},{3,11},{4,12},{5,13},{6,14},{7,15},{8,0},{9,1},... | collective-permute-start | bytes 172040 | tf_op jit(solution)/shard_map/ppermute | solution.py:63
  31.3 0.0 copy-done
  31.3 0.0 copy-done.1
  31.3 0.1 fusion
  31.4 0.1 copy.10.tables
  31.5 0.0 collective-permute-done.10.b
  31.5 0.0 collective-permute-done.11.c
  31.5 0.9 %collective-permute-done.9.a = bf16[4,7168]{1,0:T(4,128)(2,1)S(1)} collective-permute-done((bf16[4,7168]{1,0:T(4,128)(2,1)S(1)}, bf16[4,7168]{1,0:T(4,128)(2,1)S(1)}, u32[]{:S(2)}, u32[]{:S(2)}) %collective-permute-start.9) | collective-permute-done | bytes 57376 | tf_op jit(solution)/shard_map/ppermute | solution.py:63
  32.4 1.6 %collective-permute-done.15.cross = bf16[4,7168]{1,0:T(4,128)(2,1)S(1)} collective-permute-done((bf16[4,7168]{1,0:T(4,128)(2,1)S(1)}, bf16[4,7168]{1,0:T(4,128)(2,1)S(1)}, u32[]{:S(2)}, u32[]{:S(2)}) %collective-permute-start.15) | collective-permute-done | bytes 57376 | tf_op jit(solution)/shard_map/ppermute | solution.py:63
  34.0 0.7 %shard_map.79 = bf16[4,7168]{1,0:T(4,128)(2,1)} custom-call(f32[4,2]{1,0:T(4,128)S(1)} %copy.10.tables, bf16[8,4,7168]{2,1,0:T(4,128)(2,1)S(1)} %get-tuple-element.22.keep, bf16[8,4,7168]{2,1,0:T(4,128)(2,1)S(1)} %collective-permute-done.8.got, bf16[4,7168]{1,0:T(4,128)(2,1)S(1)} %collective-permute-done.9.a, bf16[4,7168]{1,0:T(4,128)(2,1)S(1)} %collective-permute-done.10.b, ...), custom_call_target="tpu_custom_call" | custom-call | tf_op jit(solution)/shard_map/pallas_call | solution.py:172
  (1 shorter events, 0.0 us)
Async XLA Ops:
  0.0 7.5 %collective-permute-start = (bf16[4,7168]{1,0:T(4,128)(2,1)}, bf16[4,7168]{1,0:T(4,128)(2,1)S(1)}, u32[]{:S(2)}, u32[]{:S(2)}) collective-permute-start(bf16[4,7168]{1,0:T(4,128)(2,1)} %refs_4_.1), channel_id=1, source_target_pairs={{0,8},{1,9},{2,10},{3,11},{4,12},{5,13},{6,14},{7,15},{8,0},{9,1},... | collective-permute-start | bytes 172040 | tf_op jit(solution)/shard_map/ppermute | solution.py:63
  4.0 6.5 %collective-permute-start.1 = (bf16[4,7168]{1,0:T(4,128)(2,1)}, bf16[4,7168]{1,0:T(4,128)(2,1)S(1)}, u32[]{:S(2)}, u32[]{:S(2)}) collective-permute-start(bf16[4,7168]{1,0:T(4,128)(2,1)} %refs_4_.1), channel_id=1, source_target_pairs={{0,2},{1,5},{2,0},{3,7},{4,6},{5,1},{6,4},{7,3},{8,10},{9,13},{10,... | collective-permute-start | bytes 172040 | tf_op jit(solution)/shard_map/ppermute | solution.py:63
  5.5 8.7 %collective-permute-start.2 = (bf16[4,7168]{1,0:T(4,128)(2,1)}, bf16[4,7168]{1,0:T(4,128)(2,1)S(1)}, u32[]{:S(2)}, u32[]{:S(2)}) collective-permute-start(bf16[4,7168]{1,0:T(4,128)(2,1)} %refs_4_.1), channel_id=1, source_target_pairs={{0,6},{1,7},{2,4},{3,5},{4,2},{5,3},{6,0},{7,1},{8,14},{9,15},{10,... | collective-permute-start | bytes 172040 | tf_op jit(solution)/shard_map/ppermute | solution.py:63
  7.1 7.2 %collective-permute-start.3 = (bf16[4,7168]{1,0:T(4,128)(2,1)}, bf16[4,7168]{1,0:T(4,128)(2,1)S(1)}, u32[]{:S(2)}, u32[]{:S(2)}) collective-permute-start(bf16[4,7168]{1,0:T(4,128)(2,1)} %refs_4_.1), channel_id=1, source_target_pairs={{0,4},{1,3},{2,6},{3,1},{4,0},{5,7},{6,2},{7,5},{8,12},{9,11},{10,... | collective-permute-start | bytes 172040 | tf_op jit(solution)/shard_map/ppermute | solution.py:63
  7.5 6.7 %collective-permute-start.4 = (bf16[4,7168]{1,0:T(4,128)(2,1)S(1)}, bf16[4,7168]{1,0:T(4,128)(2,1)S(1)}, u32[]{:S(2)}, u32[]{:S(2)}) collective-permute-start(bf16[4,7168]{1,0:T(4,128)(2,1)S(1)} %collective-permute-done.refs_0_.refs_1_), channel_id=1, source_target_pairs={{0,2},{1,5},{2,0},{3,7},{4,6},{5,1},{6,4},{7,3},{8,10},{9,13},{10,... | collective-permute-start | bytes 172040 | tf_op jit(solution)/shard_map/ppermute | solution.py:63
  9.0 5.2 %collective-permute-start.5 = (bf16[4,7168]{1,0:T(4,128)(2,1)S(1)}, bf16[4,7168]{1,0:T(4,128)(2,1)S(1)}, u32[]{:S(2)}, u32[]{:S(2)}) collective-permute-start(bf16[4,7168]{1,0:T(4,128)(2,1)S(1)} %collective-permute-done.refs_0_.refs_1_), channel_id=1, source_target_pairs={{0,6},{1,7},{2,4},{3,5},{4,2},{5,3},{6,0},{7,1},{8,14},{9,15},{10,... | collective-permute-start | bytes 172040 | tf_op jit(solution)/shard_map/ppermute | solution.py:63
  10.6 4.2 %collective-permute-start.6 = (bf16[4,7168]{1,0:T(4,128)(2,1)S(1)}, bf16[4,7168]{1,0:T(4,128)(2,1)S(1)}, u32[]{:S(2)}, u32[]{:S(2)}) collective-permute-start(bf16[4,7168]{1,0:T(4,128)(2,1)S(1)} %collective-permute-done.refs_0_.refs_1_), channel_id=1, source_target_pairs={{0,4},{1,3},{2,6},{3,1},{4,0},{5,7},{6,2},{7,5},{8,12},{9,11},{10,... | collective-permute-start | bytes 172040 | tf_op jit(solution)/shard_map/ppermute | solution.py:63
  15.2 2.1 %collective-permute-start.7 = (bf16[32,7168]{1,0:T(8,128)(2,1)S(1)}, bf16[32,7168]{1,0:T(8,128)(2,1)S(1)}, u32[]{:S(2)}, u32[]{:S(2)}) collective-permute-start(bf16[32,7168]{1,0:T(8,128)(2,1)S(1)} %shard_map.74.refs_0_), channel_id=1, source_target_pairs={{0,1},{1,0},{2,3},{3,2},{4,5},{5,4},{6,7},{7,6},{8,9},{9,8},{10,11... | collective-permute-start | bytes 1376264 | tf_op jit(solution)/shard_map/ppermute | solution.py:63
  17.3 14.0 %copy-start = (f32[4,2]{0,1:T(2,128)S(1)}, f32[4,2]{0,1:T(2,128)}, u32[]{:S(2)}) copy-start(f32[4,2]{0,1:T(2,128)} %param.10) | copy-start | bytes 100
  17.4 14.0 %copy-start.1 = (s32[4,2]{0,1:T(2,128)S(1)}, s32[4,2]{0,1:T(2,128)}, u32[]{:S(2)}) copy-start(s32[4,2]{0,1:T(2,128)} %param.9) | copy-start | bytes 100
  19.5 2.0 %collective-permute-start.8 = (bf16[8,4,7168]{2,1,0:T(4,128)(2,1)S(1)}, bf16[8,4,7168]{2,1,0:T(4,128)(2,1)S(1)}, u32[]{:S(2)}, u32[]{:S(2)}) collective-permute-start(bf16[8,4,7168]{2,1,0:T(4,128)(2,1)S(1)} %get-tuple-element.23), channel_id=1, source_target_pairs={{0,1},{1,0},{2,3},{3,2},{4,5},{5,4},{6,7},{7,6},{8,9},{9,8},{10,11... | collective-permute-start | bytes 1376264 | tf_op jit(solution)/shard_map/ppermute | solution.py:63
  21.7 6.6 %collective-permute-start.12 = (bf16[4,7168]{1,0:T(4,128)(2,1)S(1)}, bf16[4,7168]{1,0:T(4,128)(2,1)S(1)}, u32[]{:S(2)}, u32[]{:S(2)}) collective-permute-start(bf16[4,7168]{1,0:T(4,128)(2,1)S(1)} %get-tuple-element.28), channel_id=1, source_target_pairs={{0,2},{1,5},{2,0},{3,7},{4,6},{5,1},{6,4},{7,3},{8,10},{9,13},{10,... | collective-permute-start | bytes 172040 | tf_op jit(solution)/shard_map/ppermute | solution.py:63
  23.2 5.6 %collective-permute-start.13 = (bf16[4,7168]{1,0:T(4,128)(2,1)S(1)}, bf16[4,7168]{1,0:T(4,128)(2,1)S(1)}, u32[]{:S(2)}, u32[]{:S(2)}) collective-permute-start(bf16[4,7168]{1,0:T(4,128)(2,1)S(1)} %get-tuple-element.29), channel_id=1, source_target_pairs={{0,6},{1,7},{2,4},{3,5},{4,2},{5,3},{6,0},{7,1},{8,14},{9,15},{10,... | collective-permute-start | bytes 172040 | tf_op jit(solution)/shard_map/ppermute | solution.py:63
  24.3 4.5 %collective-permute-start.14 = (bf16[4,7168]{1,0:T(4,128)(2,1)S(1)}, bf16[4,7168]{1,0:T(4,128)(2,1)S(1)}, u32[]{:S(2)}, u32[]{:S(2)}) collective-permute-start(bf16[4,7168]{1,0:T(4,128)(2,1)S(1)} %get-tuple-element.30), channel_id=1, source_target_pairs={{0,4},{1,3},{2,6},{3,1},{4,0},{5,7},{6,2},{7,5},{8,12},{9,11},{10,... | collective-permute-start | bytes 172040 | tf_op jit(solution)/shard_map/ppermute | solution.py:63
  25.3 6.2 %collective-permute-start.10 = (bf16[4,7168]{1,0:T(4,128)(2,1)S(1)}, bf16[4,7168]{1,0:T(4,128)(2,1)S(1)}, u32[]{:S(2)}, u32[]{:S(2)}) collective-permute-start(bf16[4,7168]{1,0:T(4,128)(2,1)S(1)} %get-tuple-element.25), channel_id=1, source_target_pairs={{0,6},{1,7},{2,4},{3,5},{4,2},{5,3},{6,0},{7,1},{8,14},{9,15},{10,... | collective-permute-start | bytes 172040 | tf_op jit(solution)/shard_map/ppermute | solution.py:63
  27.3 4.2 %collective-permute-start.11 = (bf16[4,7168]{1,0:T(4,128)(2,1)S(1)}, bf16[4,7168]{1,0:T(4,128)(2,1)S(1)}, u32[]{:S(2)}, u32[]{:S(2)}) collective-permute-start(bf16[4,7168]{1,0:T(4,128)(2,1)S(1)} %get-tuple-element.26), channel_id=1, source_target_pairs={{0,4},{1,3},{2,6},{3,1},{4,0},{5,7},{6,2},{7,5},{8,12},{9,11},{10,... | collective-permute-start | bytes 172040 | tf_op jit(solution)/shard_map/ppermute | solution.py:63
  28.3 4.2 %collective-permute-start.9 = (bf16[4,7168]{1,0:T(4,128)(2,1)S(1)}, bf16[4,7168]{1,0:T(4,128)(2,1)S(1)}, u32[]{:S(2)}, u32[]{:S(2)}) collective-permute-start(bf16[4,7168]{1,0:T(4,128)(2,1)S(1)} %get-tuple-element.24), channel_id=1, source_target_pairs={{0,2},{1,5},{2,0},{3,7},{4,6},{5,1},{6,4},{7,3},{8,10},{9,13},{10,... | collective-permute-start | bytes 172040 | tf_op jit(solution)/shard_map/ppermute | solution.py:63
  28.9 5.2 %collective-permute-start.15 = (bf16[4,7168]{1,0:T(4,128)(2,1)S(1)}, bf16[4,7168]{1,0:T(4,128)(2,1)S(1)}, u32[]{:S(2)}, u32[]{:S(2)}) collective-permute-start(bf16[4,7168]{1,0:T(4,128)(2,1)S(1)} %shard_map.78), channel_id=1, source_target_pairs={{0,8},{1,9},{2,10},{3,11},{4,12},{5,13},{6,14},{7,15},{8,0},{9,1},... | collective-permute-start | bytes 172040 | tf_op jit(solution)/shard_map/ppermute | solution.py:63

commit v4 on v3

--- a/solution.py
+++ b/solution.py
@@ -1,5 +1,3 @@
-import functools
-
 import jax
 import jax.numpy as jnp
 from jax import lax
@@ -9,7 +7,8 @@
 
 SHARDS = 8
 CHUNKS = 4
-LINKS = ((2, 4), (6,), (4, 2))
+NEAR = ((2, 4), (4, 2), (6,))
+FAR = ((2, 4), (6,), (4, 2))
 VMEM = pl.BlockSpec(memory_space=pltpu.VMEM)
 HBM = pl.BlockSpec(memory_space=pltpu.HBM)
 SMALL = pltpu.CompilerParams(vmem_limit_bytes=4 * 1024 * 1024)
@@ -69,59 +68,66 @@
     return (values * scale * gain[...]).astype(jnp.bfloat16)
 
 
-def fetch_kernel(count, *refs):
-    sources, targets, sems = refs[1 : count + 1], refs[count + 1 : -1], refs[-1]
-    copies = [pltpu.make_async_copy(s, t, sems.at[i]) for i, (s, t) in enumerate(zip(sources, targets))]
+def first_kernel(*refs):
+    *pieces, own_hbm, gain_hbm, gate_hbm, up_hbm, normed, gain, gate_w, up_w, own, sems = refs
+    pairs = ((own_hbm, own), (gain_hbm, gain), (gate_hbm, gate_w), (up_hbm, up_w))
+    copies = [pltpu.make_async_copy(s, t, sems.at[i]) for i, (s, t) in enumerate(pairs)]
     for copy in copies:
         copy.start()
-    for copy in copies:
-        copy.wait()
+    copies[0].wait()
+    copies[1].wait()
+    tok = own.shape[0]
+    for k, piece in enumerate((own, *pieces)):
+        normed[tok * k : tok * (k + 1), :] = rows_normed(piece, gain)
+    copies[2].wait()
+    copies[3].wait()
+
+
+def first_call(pieces, own, gain, *weights):
+    read = sum(w.size * w.dtype.itemsize for w in weights)
+    tok, width = own.shape
+    shapes = ((tok * (len(pieces) + 1), width), gain.shape, *(w.shape for w in weights))
+    kinds = (jnp.bfloat16, gain.dtype, *(w.dtype for w in weights))
+    return pl.pallas_call(
+        first_kernel,
+        out_shape=tuple(pltpu.VMEM(shape, kind) for shape, kind in zip(shapes, kinds)),
+        in_specs=[VMEM] * len(pieces) + [HBM] * 4,
+        out_specs=(VMEM,) * 4,
+        scratch_shapes=[pltpu.VMEM((tok, width), jnp.bfloat16), pltpu.SemaphoreType.DMA((4,))],
+        compiler_params=SMALL,
+        cost_estimate=pl.CostEstimate(flops=0, bytes_accessed=2 * read, transcendentals=0),
+    )(*pieces, *[in_hbm(a) for a in (own, gain, *weights)])
 
 
 def in_hbm(array):
     return pltpu.with_memory_space_constraint(array, pltpu.HBM)
 
 
-def fetch_call(after, *arrays):
-    count = len(arrays)
-    read = sum(a.size * a.dtype.itemsize for a in arrays)
-    return pl.pallas_call(
-        functools.partial(fetch_kernel, count),
-        out_shape=tuple(pltpu.VMEM(a.shape, a.dtype) for a in arrays),
-        in_specs=[VMEM] + [HBM] * count,
-        out_specs=(VMEM,) * count,
-        scratch_shapes=[pltpu.SemaphoreType.DMA((count,))],
-        compiler_params=SMALL,
-        cost_estimate=pl.CostEstimate(flops=0, bytes_accessed=2 * read, transcendentals=0),
-    )(after, *[in_hbm(a) for a in arrays])
-
-
-def norm_kernel(gain, *refs):
+def norm_kernel(gain, early, *refs):
     normed = refs[-1]
     tok = refs[0].shape[0]
+    done = early.shape[0]
+    normed[:done, :] = early[...]
     for k, piece in enumerate(refs[:-1]):
-        normed[tok * k : tok * (k + 1), :] = rows_normed(piece, gain)
-
-
-def norm_call(gain, pieces):
+        normed[done + tok * k : done + tok * (k + 1), :] = rows_normed(piece, gain)
+
+
+def norm_call(gain, early, pieces):
     tok, width = pieces[0].shape
     return pl.pallas_call(
         norm_kernel,
-        out_shape=jax.ShapeDtypeStruct((tok * len(pieces), width), jnp.bfloat16),
-        in_specs=[VMEM] * (len(pieces) + 1),
+        out_shape=jax.ShapeDtypeStruct((early.shape[0] + tok * len(pieces), width), jnp.bfloat16),
+        in_specs=[VMEM] * (len(pieces) + 2),
         out_specs=VMEM,
         compiler_params=SMALL,
-    )(gain, *pieces)
+    )(gain, early, *pieces)
 
 
 def expert_kernel(*refs):
-    *parts, gate_w, up_w, down_w, keep, give, normed = refs
-    row = 0
-    for part in parts:
-        normed[row : row + part.shape[0], :] = part[...]
-        row += part.shape[0]
-    gate = jnp.dot(normed[...], gate_w[0], preferred_element_type=jnp.float32)
-    upper = jnp.dot(normed[...], up_w[0], preferred_element_type=jnp.float32)
+    *parts, gate_w, up_w, down_w, keep, give = refs
+    rows = jnp.concatenate([part[...] for part in parts], axis=0)
+    gate = jnp.dot(rows, gate_w[0], preferred_element_type=jnp.float32)
+    upper = jnp.dot(rows, up_w[0], preferred_element_type=jnp.float32)
     active = (gate / (1.0 + jnp.exp(-gate)) * upper).astype(jnp.bfloat16)
     step = down_w.shape[2] // CHUNKS
     for c in range(CHUNKS):
@@ -142,7 +148,6 @@
         out_shape=(half, half),
         in_specs=[VMEM] * (len(parts) + 3),
         out_specs=(VMEM, VMEM),
-        scratch_shapes=[pltpu.VMEM((2 * rows, width), jnp.bfloat16)],
         compiler_params=pltpu.CompilerParams(vmem_limit_bytes=16 * 1024 * 1024),
     )(*parts, *weights)
 
@@ -183,18 +188,17 @@
     x = hidden_rows
     gain = norm_gain[None, :]
     far_rows = swap(x, 8)
-    near_pieces = [swap(x, *masks) for masks in LINKS]
-    far_pieces = [swap(far_rows, *masks) for masks in LINKS]
-    gate_w, up_w, gain, own = fetch_call(far_rows, gate_weight, up_weight, gain, x)
-    rows = norm_call(gain, [own, far_rows, *near_pieces, *far_pieces])
-    (down_w,) = fetch_call(rows, down_weight)
-    keep, give = experts_call(x.shape[0], (rows, swap(rows, 1)), (gate_w, up_w, down_w))
+    near_pieces = [swap(x, *masks) for masks in NEAR]
+    far_pieces = [swap(far_rows, *masks) for masks in FAR]
+    early, gain, gate_w, up_w = first_call([far_rows, *near_pieces[:2]], x, gain, gate_weight, up_weight)
+    rows = norm_call(gain, early, near_pieces[2:] + far_pieces)
+    keep, give = experts_call(x.shape[0], (rows, swap(rows, 1)), (gate_w, up_w, down_weight))
     got = swap(give, 1)
     block = jax.ShapeDtypeStruct(x.shape, jnp.bfloat16)
     sums = small_call(pair_kernel, 7, block, keep, got)
-    far = [swap(part, *masks) for part, masks in zip(sums[4:], LINKS)]
+    far = [swap(part, *masks) for part, masks in zip(sums[4:], FAR)]
     cross = swap(small_call(across_kernel, 1, block, sums[0], *far), 8)
-    near = [swap(part, *masks) for part, masks in zip(sums[1:4], LINKS)]
+    near = [swap(part, *masks) for part, masks in zip(sums[1:4], NEAR)]
     return small_call(last_kernel, 1, block, table, keep, got, *near, cross)
 
 

time: 34.9 us -> 34.4 us (0.986)
  Pallas kernels: 8.76 us -> 6.7 us
  waiting for transfers between devices: 4.47 us -> 6.44 us
    pallas_call x3 -> x2, Pallas kernels: 5.69 us -> 3.63 us  [the longest x1 3.38 us: first_call(): pl.pallas_call(first_kernel, out_shape=tuple((pltpu.VMEM(shape, kind) for...]
    ppermute x16, waiting for transfers between devices: 4.47 us -> 6.44 us  [swap(): lax.ppermute(array, 'expert', [(i, i ^ masks[i % len(masks)]) for i in ra...]
  transfers between devices with their start and end apart: 16 -> 16, of which waited for: 4 -> 7; matrix products, arithmetic and copies ran while one was open for 1% -> 1% of each run, Pallas kernels for 15% -> 10%
where the time goes in v4:
time: 34.4 us; the launch traced here: 34.3 us
  starting transfers between devices  20.8 us (60%)
  Pallas kernels  6.7 us (19%)
  waiting for transfers between devices  6.44 us (19%)
    ppermute x16, starting transfers between devices, swap(): lax.ppermute(array, 'expert', [(i, i ^ masks[i % len(masks)]) for i in ra...  20.8 us
    ppermute x16, waiting for transfers between devices, swap(): lax.ppermute(array, 'expert', [(i, i ^ masks[i % len(masks)]) for i in ra...  6.44 us
    pallas_call x1, Pallas kernels, first_call(): pl.pallas_call(first_kernel, out_shape=tuple((pltpu.VMEM(shape, kind) for...  3.38 us
    pallas_call x1, Pallas kernels, experts_call(): pl.pallas_call(expert_kernel, out_shape=(half, half), in_specs=[VMEM] * (...  2.11 us
    pallas_call x3, Pallas kernels, small_call(): pl.pallas_call(kernel, out_shape=shape, in_specs=[VMEM] * len(operands),...  0.96 us
  transfers between devices with their start and end apart: 16, of which 7 were waited for; matrix products, arithmetic and copies ran while one was open for 1% of the time, Pallas kernels for 10%

profile of v4, /device:TPU:0, one launch (start us, length us, event | category | flops | bytes accessed | tf_op | source)
XLA Modules:
  0.0 34.3 jit_solution(11078054682187698952)
XLA Ops:
  0.0 4.0 %collective-permute-start = (bf16[4,7168]{1,0:T(4,128)(2,1)}, bf16[4,7168]{1,0:T(4,128)(2,1)S(1)}, u32[]{:S(2)}, u32[]{:S(2)}) collective-permute-start(bf16[4,7168]{1,0:T(4,128)(2,1)} %refs_3_.1), channel_id=1, source_target_pairs={{0,8},{1,9},{2,10},{3,11},{4,12},{5,13},{6,14},{7,15},{8,0},{9,1},... | collective-permute-start | bytes 172040 | tf_op jit(solution)/shard_map/ppermute | solution.py:62
  4.0 1.5 %collective-permute-start.1 = (bf16[4,7168]{1,0:T(4,128)(2,1)}, bf16[4,7168]{1,0:T(4,128)(2,1)S(1)}, u32[]{:S(2)}, u32[]{:S(2)}) collective-permute-start(bf16[4,7168]{1,0:T(4,128)(2,1)} %refs_3_.1), channel_id=1, source_target_pairs={{0,2},{1,5},{2,0},{3,7},{4,6},{5,1},{6,4},{7,3},{8,10},{9,13},{10,... | collective-permute-start | bytes 172040 | tf_op jit(solution)/shard_map/ppermute | solution.py:62
  5.5 1.6 %collective-permute-start.2 = (bf16[4,7168]{1,0:T(4,128)(2,1)}, bf16[4,7168]{1,0:T(4,128)(2,1)S(1)}, u32[]{:S(2)}, u32[]{:S(2)}) collective-permute-start(bf16[4,7168]{1,0:T(4,128)(2,1)} %refs_3_.1), channel_id=1, source_target_pairs={{0,4},{1,3},{2,6},{3,1},{4,0},{5,7},{6,2},{7,5},{8,12},{9,11},{10,... | collective-permute-start | bytes 172040 | tf_op jit(solution)/shard_map/ppermute | solution.py:62
  7.1 0.4 %collective-permute-start.3 = (bf16[4,7168]{1,0:T(4,128)(2,1)}, bf16[4,7168]{1,0:T(4,128)(2,1)S(1)}, u32[]{:S(2)}, u32[]{:S(2)}) collective-permute-start(bf16[4,7168]{1,0:T(4,128)(2,1)} %refs_3_.1), channel_id=1, source_target_pairs={{0,6},{1,7},{2,4},{3,5},{4,2},{5,3},{6,0},{7,1},{8,14},{9,15},{10,... | collective-permute-start | bytes 172040 | tf_op jit(solution)/shard_map/ppermute | solution.py:62
  7.5 0.0 collective-permute-done.refs_0_
  7.5 1.5 %collective-permute-start.4 = (bf16[4,7168]{1,0:T(4,128)(2,1)S(1)}, bf16[4,7168]{1,0:T(4,128)(2,1)S(1)}, u32[]{:S(2)}, u32[]{:S(2)}) collective-permute-start(bf16[4,7168]{1,0:T(4,128)(2,1)S(1)} %collective-permute-done.refs_0_), channel_id=1, source_target_pairs={{0,2},{1,5},{2,0},{3,7},{4,6},{5,1},{6,4},{7,3},{8,10},{9,13},{10,... | collective-permute-start | bytes 172040 | tf_op jit(solution)/shard_map/ppermute | solution.py:62
  9.0 1.5 %collective-permute-start.5 = (bf16[4,7168]{1,0:T(4,128)(2,1)S(1)}, bf16[4,7168]{1,0:T(4,128)(2,1)S(1)}, u32[]{:S(2)}, u32[]{:S(2)}) collective-permute-start(bf16[4,7168]{1,0:T(4,128)(2,1)S(1)} %collective-permute-done.refs_0_), channel_id=1, source_target_pairs={{0,6},{1,7},{2,4},{3,5},{4,2},{5,3},{6,0},{7,1},{8,14},{9,15},{10,... | collective-permute-start | bytes 172040 | tf_op jit(solution)/shard_map/ppermute | solution.py:62
  10.6 0.0 collective-permute-done.1.refs_1_
  10.6 0.5 %collective-permute-start.6 = (bf16[4,7168]{1,0:T(4,128)(2,1)S(1)}, bf16[4,7168]{1,0:T(4,128)(2,1)S(1)}, u32[]{:S(2)}, u32[]{:S(2)}) collective-permute-start(bf16[4,7168]{1,0:T(4,128)(2,1)S(1)} %collective-permute-done.refs_0_), channel_id=1, source_target_pairs={{0,4},{1,3},{2,6},{3,1},{4,0},{5,7},{6,2},{7,5},{8,12},{9,11},{10,... | collective-permute-start | bytes 172040 | tf_op jit(solution)/shard_map/ppermute | solution.py:62
  11.0 0.0 collective-permute-done.2.refs_2_
  11.0 0.0 copy-start
  11.0 3.4 %shard_map.73 = (bf16[16,7168]{1,0:T(8,128)(2,1)S(1)}, f32[1,7168]{1,0:T(1,128)S(1)}, bf16[1,7168,256]{2,1,0:T(8,128)(2,1)S(1)}, bf16[1,7168,256]{2,1,0:T(8,128)(2,1)S(1)}) custom-call(bf16[4,7168]{1,0:T(4,128)(2,1)S(1)} %collective-permute-done.refs_0_, bf16[4,7168]{1,0:T(4,128)(2,1)S(1)} %collective-permute-done.1.refs_1_, ...), custom_call_target="tpu_custom_call" | custom-call | bytes 14680064 | tf_op jit(solution)/shard_map/pallas_call | solution.py:91
  14.4 0.0 collective-permute-done.3.refs_0_
  14.4 0.0 collective-permute-done.4.refs_1_
  14.4 0.0 collective-permute-done.5.refs_2_
  14.4 0.3 collective-permute-done.6.refs_3_
  14.8 0.3 shard_map.74.refs_0_
  15.0 0.1 collective-permute-start.7
  15.1 1.8 %collective-permute-done.7.refs_1_ = bf16[32,7168]{1,0:T(8,128)(2,1)S(1)} collective-permute-done((bf16[32,7168]{1,0:T(8,128)(2,1)S(1)}, bf16[32,7168]{1,0:T(8,128)(2,1)S(1)}, u32[]{:S(2)}, u32[]{:S(2)}) %collective-permute-start.7) | collective-permute-done | bytes 458784 | tf_op jit(solution)/shard_map/ppermute | solution.py:62
  16.9 0.0 copy-done
  16.9 0.0 copy-start.1
  16.9 0.0 copy-start.2
  16.9 2.1 %shard_map.75 = (bf16[8,4,7168]{2,1,0:T(4,128)(2,1)S(1)}, bf16[8,4,7168]{2,1,0:T(4,128)(2,1)S(1)}) custom-call(bf16[32,7168]{1,0:T(8,128)(2,1)S(1)} %shard_map.74.refs_0_, bf16[32,7168]{1,0:T(8,128)(2,1)S(1)} %collective-permute-done.7.refs_1_, bf16[1,7168,256]{2,1,0:T(8,128)(2,1)S(1)} %get-tuple-element.20.refs_2_, ...), custom_call_target="tpu_custom_call" | custom-call | tf_op jit(solution)/shard_map/pallas_call | solution.py:146
  19.0 0.2 collective-permute-start.8
  19.2 1.7 %collective-permute-done.8.got = bf16[8,4,7168]{2,1,0:T(4,128)(2,1)S(1)} collective-permute-done((bf16[8,4,7168]{2,1,0:T(4,128)(2,1)S(1)}, bf16[8,4,7168]{2,1,0:T(4,128)(2,1)S(1)}, u32[]{:S(2)}, u32[]{:S(2)}) %collective-permute-start.8) | collective-permute-done | bytes 458784 | tf_op jit(solution)/shard_map/ppermute | solution.py:62
  20.9 0.2 shard_map.76
  21.1 1.6 %collective-permute-start.12 = (bf16[4,7168]{1,0:T(4,128)(2,1)S(1)}, bf16[4,7168]{1,0:T(4,128)(2,1)S(1)}, u32[]{:S(2)}, u32[]{:S(2)}) collective-permute-start(bf16[4,7168]{1,0:T(4,128)(2,1)S(1)} %get-tuple-element.28), channel_id=1, source_target_pairs={{0,2},{1,5},{2,0},{3,7},{4,6},{5,1},{6,4},{7,3},{8,10},{9,13},{10,... | collective-permute-start | bytes 172040 | tf_op jit(solution)/shard_map/ppermute | solution.py:62
  22.6 1.3 %collective-permute-start.13 = (bf16[4,7168]{1,0:T(4,128)(2,1)S(1)}, bf16[4,7168]{1,0:T(4,128)(2,1)S(1)}, u32[]{:S(2)}, u32[]{:S(2)}) collective-permute-start(bf16[4,7168]{1,0:T(4,128)(2,1)S(1)} %get-tuple-element.29), channel_id=1, source_target_pairs={{0,6},{1,7},{2,4},{3,5},{4,2},{5,3},{6,0},{7,1},{8,14},{9,15},{10,... | collective-permute-start | bytes 172040 | tf_op jit(solution)/shard_map/ppermute | solution.py:62
  23.9 0.7 %collective-permute-start.14 = (bf16[4,7168]{1,0:T(4,128)(2,1)S(1)}, bf16[4,7168]{1,0:T(4,128)(2,1)S(1)}, u32[]{:S(2)}, u32[]{:S(2)}) collective-permute-start(bf16[4,7168]{1,0:T(4,128)(2,1)S(1)} %get-tuple-element.30), channel_id=1, source_target_pairs={{0,4},{1,3},{2,6},{3,1},{4,0},{5,7},{6,2},{7,5},{8,12},{9,11},{10,... | collective-permute-start | bytes 172040 | tf_op jit(solution)/shard_map/ppermute | solution.py:62
  24.6 0.1 pad_add_fusion
  24.7 1.3 %collective-permute-start.10 = (bf16[4,7168]{1,0:T(4,128)(2,1)S(1)}, bf16[4,7168]{1,0:T(4,128)(2,1)S(1)}, u32[]{:S(2)}, u32[]{:S(2)}) collective-permute-start(bf16[4,7168]{1,0:T(4,128)(2,1)S(1)} %get-tuple-element.25), channel_id=1, source_target_pairs={{0,4},{1,3},{2,6},{3,1},{4,0},{5,7},{6,2},{7,5},{8,12},{9,11},{10,... | collective-permute-start | bytes 172040 | tf_op jit(solution)/shard_map/ppermute | solution.py:62
  26.0 1.7 %collective-permute-start.11 = (bf16[4,7168]{1,0:T(4,128)(2,1)S(1)}, bf16[4,7168]{1,0:T(4,128)(2,1)S(1)}, u32[]{:S(2)}, u32[]{:S(2)}) collective-permute-start(bf16[4,7168]{1,0:T(4,128)(2,1)S(1)} %get-tuple-element.26), channel_id=1, source_target_pairs={{0,6},{1,7},{2,4},{3,5},{4,2},{5,3},{6,0},{7,1},{8,14},{9,15},{10,... | collective-permute-start | bytes 172040 | tf_op jit(solution)/shard_map/ppermute | solution.py:62
  27.7 0.0 collective-permute-done.12.a
  27.7 0.5 %collective-permute-start.9 = (bf16[4,7168]{1,0:T(4,128)(2,1)S(1)}, bf16[4,7168]{1,0:T(4,128)(2,1)S(1)}, u32[]{:S(2)}, u32[]{:S(2)}) collective-permute-start(bf16[4,7168]{1,0:T(4,128)(2,1)S(1)} %get-tuple-element.24), channel_id=1, source_target_pairs={{0,2},{1,5},{2,0},{3,7},{4,6},{5,1},{6,4},{7,3},{8,10},{9,13},{10,... | collective-permute-start | bytes 172040 | tf_op jit(solution)/shard_map/ppermute | solution.py:62
  28.2 0.0 collective-permute-done.13.b
  28.2 0.2 collective-permute-done.14.c
  28.4 2.5 %collective-permute-start.15 = (bf16[4,7168]{1,0:T(4,128)(2,1)S(1)}, bf16[4,7168]{1,0:T(4,128)(2,1)S(1)}, u32[]{:S(2)}, u32[]{:S(2)}) collective-permute-start(bf16[4,7168]{1,0:T(4,128)(2,1)S(1)} %shard_map.77), channel_id=1, source_target_pairs={{0,8},{1,9},{2,10},{3,11},{4,12},{5,13},{6,14},{7,15},{8,0},{9,1},... | collective-permute-start | bytes 172040 | tf_op jit(solution)/shard_map/ppermute | solution.py:62
  30.9 0.0 copy-done.1
  30.9 0.0 copy-done.2
  30.9 0.1 fusion
  31.0 0.1 copy.10.tables
  31.1 0.0 collective-permute-done.10.b
  31.1 0.4 %collective-permute-done.11.c = bf16[4,7168]{1,0:T(4,128)(2,1)S(1)} collective-permute-done((bf16[4,7168]{1,0:T(4,128)(2,1)S(1)}, bf16[4,7168]{1,0:T(4,128)(2,1)S(1)}, u32[]{:S(2)}, u32[]{:S(2)}) %collective-permute-start.11) | collective-permute-done | bytes 57376 | tf_op jit(solution)/shard_map/ppermute | solution.py:62
  31.5 0.6 %collective-permute-done.9.a = bf16[4,7168]{1,0:T(4,128)(2,1)S(1)} collective-permute-done((bf16[4,7168]{1,0:T(4,128)(2,1)S(1)}, bf16[4,7168]{1,0:T(4,128)(2,1)S(1)}, u32[]{:S(2)}, u32[]{:S(2)}) %collective-permute-start.9) | collective-permute-done | bytes 57376 | tf_op jit(solution)/shard_map/ppermute | solution.py:62
  32.1 1.5 %collective-permute-done.15.cross = bf16[4,7168]{1,0:T(4,128)(2,1)S(1)} collective-permute-done((bf16[4,7168]{1,0:T(4,128)(2,1)S(1)}, bf16[4,7168]{1,0:T(4,128)(2,1)S(1)}, u32[]{:S(2)}, u32[]{:S(2)}) %collective-permute-start.15) | collective-permute-done | bytes 57376 | tf_op jit(solution)/shard_map/ppermute | solution.py:62
  33.6 0.7 %shard_map.78 = bf16[4,7168]{1,0:T(4,128)(2,1)} custom-call(f32[4,2]{1,0:T(4,128)S(1)} %copy.10.tables, bf16[8,4,7168]{2,1,0:T(4,128)(2,1)S(1)} %get-tuple-element.22.keep, bf16[8,4,7168]{2,1,0:T(4,128)(2,1)S(1)} %collective-permute-done.8.got, bf16[4,7168]{1,0:T(4,128)(2,1)S(1)} %collective-permute-done.9.a, bf16[4,7168]{1,0:T(4,128)(2,1)S(1)} %collective-permute-done.10.b, ...), custom_call_target="tpu_custom_call" | custom-call | tf_op jit(solution)/shard_map/pallas_call | solution.py:177
  (1 shorter events, 0.0 us)
Async XLA Ops:
  0.0 7.5 %collective-permute-start = (bf16[4,7168]{1,0:T(4,128)(2,1)}, bf16[4,7168]{1,0:T(4,128)(2,1)S(1)}, u32[]{:S(2)}, u32[]{:S(2)}) collective-permute-start(bf16[4,7168]{1,0:T(4,128)(2,1)} %refs_3_.1), channel_id=1, source_target_pairs={{0,8},{1,9},{2,10},{3,11},{4,12},{5,13},{6,14},{7,15},{8,0},{9,1},... | collective-permute-start | bytes 172040 | tf_op jit(solution)/shard_map/ppermute | solution.py:62
  4.0 6.5 %collective-permute-start.1 = (bf16[4,7168]{1,0:T(4,128)(2,1)}, bf16[4,7168]{1,0:T(4,128)(2,1)S(1)}, u32[]{:S(2)}, u32[]{:S(2)}) collective-permute-start(bf16[4,7168]{1,0:T(4,128)(2,1)} %refs_3_.1), channel_id=1, source_target_pairs={{0,2},{1,5},{2,0},{3,7},{4,6},{5,1},{6,4},{7,3},{8,10},{9,13},{10,... | collective-permute-start | bytes 172040 | tf_op jit(solution)/shard_map/ppermute | solution.py:62
  5.5 5.5 %collective-permute-start.2 = (bf16[4,7168]{1,0:T(4,128)(2,1)}, bf16[4,7168]{1,0:T(4,128)(2,1)S(1)}, u32[]{:S(2)}, u32[]{:S(2)}) collective-permute-start(bf16[4,7168]{1,0:T(4,128)(2,1)} %refs_3_.1), channel_id=1, source_target_pairs={{0,4},{1,3},{2,6},{3,1},{4,0},{5,7},{6,2},{7,5},{8,12},{9,11},{10,... | collective-permute-start | bytes 172040 | tf_op jit(solution)/shard_map/ppermute | solution.py:62
  7.1 7.3 %collective-permute-start.3 = (bf16[4,7168]{1,0:T(4,128)(2,1)}, bf16[4,7168]{1,0:T(4,128)(2,1)S(1)}, u32[]{:S(2)}, u32[]{:S(2)}) collective-permute-start(bf16[4,7168]{1,0:T(4,128)(2,1)} %refs_3_.1), channel_id=1, source_target_pairs={{0,6},{1,7},{2,4},{3,5},{4,2},{5,3},{6,0},{7,1},{8,14},{9,15},{10,... | collective-permute-start | bytes 172040 | tf_op jit(solution)/shard_map/ppermute | solution.py:62
  7.5 6.9 %collective-permute-start.4 = (bf16[4,7168]{1,0:T(4,128)(2,1)S(1)}, bf16[4,7168]{1,0:T(4,128)(2,1)S(1)}, u32[]{:S(2)}, u32[]{:S(2)}) collective-permute-start(bf16[4,7168]{1,0:T(4,128)(2,1)S(1)} %collective-permute-done.refs_0_), channel_id=1, source_target_pairs={{0,2},{1,5},{2,0},{3,7},{4,6},{5,1},{6,4},{7,3},{8,10},{9,13},{10,... | collective-permute-start | bytes 172040 | tf_op jit(solution)/shard_map/ppermute | solution.py:62
  9.0 5.4 %collective-permute-start.5 = (bf16[4,7168]{1,0:T(4,128)(2,1)S(1)}, bf16[4,7168]{1,0:T(4,128)(2,1)S(1)}, u32[]{:S(2)}, u32[]{:S(2)}) collective-permute-start(bf16[4,7168]{1,0:T(4,128)(2,1)S(1)} %collective-permute-done.refs_0_), channel_id=1, source_target_pairs={{0,6},{1,7},{2,4},{3,5},{4,2},{5,3},{6,0},{7,1},{8,14},{9,15},{10,... | collective-permute-start | bytes 172040 | tf_op jit(solution)/shard_map/ppermute | solution.py:62
  10.6 4.2 %collective-permute-start.6 = (bf16[4,7168]{1,0:T(4,128)(2,1)S(1)}, bf16[4,7168]{1,0:T(4,128)(2,1)S(1)}, u32[]{:S(2)}, u32[]{:S(2)}) collective-permute-start(bf16[4,7168]{1,0:T(4,128)(2,1)S(1)} %collective-permute-done.refs_0_), channel_id=1, source_target_pairs={{0,4},{1,3},{2,6},{3,1},{4,0},{5,7},{6,2},{7,5},{8,12},{9,11},{10,... | collective-permute-start | bytes 172040 | tf_op jit(solution)/shard_map/ppermute | solution.py:62
  11.0 5.9 %copy-start = (bf16[1,256,7168]{2,1,0:T(8,128)(2,1)S(1)}, bf16[1,256,7168]{2,1,0:T(8,128)(2,1)}, u32[]{:S(2)}) copy-start(bf16[1,256,7168]{2,1,0:T(8,128)(2,1)} %refs_4_.1) | copy-start | bytes 11010052
  15.0 1.9 %collective-permute-start.7 = (bf16[32,7168]{1,0:T(8,128)(2,1)S(1)}, bf16[32,7168]{1,0:T(8,128)(2,1)S(1)}, u32[]{:S(2)}, u32[]{:S(2)}) collective-permute-start(bf16[32,7168]{1,0:T(8,128)(2,1)S(1)} %shard_map.74.refs_0_), channel_id=1, source_target_pairs={{0,1},{1,0},{2,3},{3,2},{4,5},{5,4},{6,7},{7,6},{8,9},{9,8},{10,11... | collective-permute-start | bytes 1376264 | tf_op jit(solution)/shard_map/ppermute | solution.py:62
  16.9 14.0 %copy-start.1 = (f32[4,2]{0,1:T(2,128)S(1)}, f32[4,2]{0,1:T(2,128)}, u32[]{:S(2)}) copy-start(f32[4,2]{0,1:T(2,128)} %param.10) | copy-start | bytes 100
  16.9 14.0 %copy-start.2 = (s32[4,2]{0,1:T(2,128)S(1)}, s32[4,2]{0,1:T(2,128)}, u32[]{:S(2)}) copy-start(s32[4,2]{0,1:T(2,128)} %param.9) | copy-start | bytes 100
  19.0 1.9 %collective-permute-start.8 = (bf16[8,4,7168]{2,1,0:T(4,128)(2,1)S(1)}, bf16[8,4,7168]{2,1,0:T(4,128)(2,1)S(1)}, u32[]{:S(2)}, u32[]{:S(2)}) collective-permute-start(bf16[8,4,7168]{2,1,0:T(4,128)(2,1)S(1)} %get-tuple-element.23), channel_id=1, source_target_pairs={{0,1},{1,0},{2,3},{3,2},{4,5},{5,4},{6,7},{7,6},{8,9},{9,8},{10,11... | collective-permute-start | bytes 1376264 | tf_op jit(solution)/shard_map/ppermute | solution.py:62
  21.1 6.6 %collective-permute-start.12 = (bf16[4,7168]{1,0:T(4,128)(2,1)S(1)}, bf16[4,7168]{1,0:T(4,128)(2,1)S(1)}, u32[]{:S(2)}, u32[]{:S(2)}) collective-permute-start(bf16[4,7168]{1,0:T(4,128)(2,1)S(1)} %get-tuple-element.28), channel_id=1, source_target_pairs={{0,2},{1,5},{2,0},{3,7},{4,6},{5,1},{6,4},{7,3},{8,10},{9,13},{10,... | collective-permute-start | bytes 172040 | tf_op jit(solution)/shard_map/ppermute | solution.py:62
  22.6 5.6 %collective-permute-start.13 = (bf16[4,7168]{1,0:T(4,128)(2,1)S(1)}, bf16[4,7168]{1,0:T(4,128)(2,1)S(1)}, u32[]{:S(2)}, u32[]{:S(2)}) collective-permute-start(bf16[4,7168]{1,0:T(4,128)(2,1)S(1)} %get-tuple-element.29), channel_id=1, source_target_pairs={{0,6},{1,7},{2,4},{3,5},{4,2},{5,3},{6,0},{7,1},{8,14},{9,15},{10,... | collective-permute-start | bytes 172040 | tf_op jit(solution)/shard_map/ppermute | solution.py:62
  23.9 4.5 %collective-permute-start.14 = (bf16[4,7168]{1,0:T(4,128)(2,1)S(1)}, bf16[4,7168]{1,0:T(4,128)(2,1)S(1)}, u32[]{:S(2)}, u32[]{:S(2)}) collective-permute-start(bf16[4,7168]{1,0:T(4,128)(2,1)S(1)} %get-tuple-element.30), channel_id=1, source_target_pairs={{0,4},{1,3},{2,6},{3,1},{4,0},{5,7},{6,2},{7,5},{8,12},{9,11},{10,... | collective-permute-start | bytes 172040 | tf_op jit(solution)/shard_map/ppermute | solution.py:62
  24.7 6.4 %collective-permute-start.10 = (bf16[4,7168]{1,0:T(4,128)(2,1)S(1)}, bf16[4,7168]{1,0:T(4,128)(2,1)S(1)}, u32[]{:S(2)}, u32[]{:S(2)}) collective-permute-start(bf16[4,7168]{1,0:T(4,128)(2,1)S(1)} %get-tuple-element.25), channel_id=1, source_target_pairs={{0,4},{1,3},{2,6},{3,1},{4,0},{5,7},{6,2},{7,5},{8,12},{9,11},{10,... | collective-permute-start | bytes 172040 | tf_op jit(solution)/shard_map/ppermute | solution.py:62
  26.0 5.5 %collective-permute-start.11 = (bf16[4,7168]{1,0:T(4,128)(2,1)S(1)}, bf16[4,7168]{1,0:T(4,128)(2,1)S(1)}, u32[]{:S(2)}, u32[]{:S(2)}) collective-permute-start(bf16[4,7168]{1,0:T(4,128)(2,1)S(1)} %get-tuple-element.26), channel_id=1, source_target_pairs={{0,6},{1,7},{2,4},{3,5},{4,2},{5,3},{6,0},{7,1},{8,14},{9,15},{10,... | collective-permute-start | bytes 172040 | tf_op jit(solution)/shard_map/ppermute | solution.py:62
  27.7 4.4 %collective-permute-start.9 = (bf16[4,7168]{1,0:T(4,128)(2,1)S(1)}, bf16[4,7168]{1,0:T(4,128)(2,1)S(1)}, u32[]{:S(2)}, u32[]{:S(2)}) collective-permute-start(bf16[4,7168]{1,0:T(4,128)(2,1)S(1)} %get-tuple-element.24), channel_id=1, source_target_pairs={{0,2},{1,5},{2,0},{3,7},{4,6},{5,1},{6,4},{7,3},{8,10},{9,13},{10,... | collective-permute-start | bytes 172040 | tf_op jit(solution)/shard_map/ppermute | solution.py:62
  28.4 5.2 %collective-permute-start.15 = (bf16[4,7168]{1,0:T(4,128)(2,1)S(1)}, bf16[4,7168]{1,0:T(4,128)(2,1)S(1)}, u32[]{:S(2)}, u32[]{:S(2)}) collective-permute-start(bf16[4,7168]{1,0:T(4,128)(2,1)S(1)} %shard_map.77), channel_id=1, source_target_pairs={{0,8},{1,9},{2,10},{3,11},{4,12},{5,13},{6,14},{7,15},{8,0},{9,1},... | collective-permute-start | bytes 172040 | tf_op jit(solution)/shard_map/ppermute | solution.py:62

commit v5 on v4

--- a/solution.py
+++ b/solution.py
@@ -165,10 +165,9 @@
     total[...] = (add(own[...], a[...]) + add(b[...], c[...])).astype(jnp.bfloat16)
 
 
-def last_kernel(tables, keep, got, a, b, c, cross, out):
+def own_kernel(tables, keep, got, a, b, c, out):
     own = add(keep[0], got[0]) + (add(a[...], b[...]) + c[...].astype(jnp.float32))
-    weight = tables[...]
-    out[...] = (weight[:, 0:1] * own + weight[:, 1:2] * cross[...].astype(jnp.float32)).astype(jnp.bfloat16)
+    out[...] = tables[...][:, 0:1] * own
 
 
 def small_call(kernel, outs, block, *operands):
@@ -199,7 +198,9 @@
     far = [swap(part, *masks) for part, masks in zip(sums[4:], FAR)]
     cross = swap(small_call(across_kernel, 1, block, sums[0], *far), 8)
     near = [swap(part, *masks) for part, masks in zip(sums[1:4], NEAR)]
-    return small_call(last_kernel, 1, block, table, keep, got, *near, cross)
+    wide = jax.ShapeDtypeStruct(x.shape, jnp.float32)
+    own = small_call(own_kernel, 1, wide, table, keep, got, *near)
+    return (own + table[:, 1:2] * cross.astype(jnp.float32)).astype(jnp.bfloat16)
 
 
 def body(*args):

time: 34.4 us -> 34.4 us (level)
  other arithmetic: 0.15 us -> 0.87 us
  Pallas kernels: 6.7 us -> 6.05 us
    convert_element_type x0 -> x1, other arithmetic: none -> 0.72 us  [dense_body(): (own + table[:, 1:2] * cross.astype(jnp.float32)).astype(jnp.bfloat16)]
    pallas_call x3, Pallas kernels: 0.96 us -> 0.31 us  [small_call(): pl.pallas_call(kernel, out_shape=shape, in_specs=[VMEM] * len(operands),...]
where the time goes in v5:
time: 34.4 us; the launch traced here: 34.3 us
  starting transfers between devices  20.8 us (60%)
  waiting for transfers between devices  6.35 us (18%)
  Pallas kernels  6.05 us (18%)
  other arithmetic  0.87 us (3%)
    ppermute x16, starting transfers between devices, swap(): lax.ppermute(array, 'expert', [(i, i ^ masks[i % len(masks)]) for i in ra...  20.8 us
    ppermute x16, waiting for transfers between devices, swap(): lax.ppermute(array, 'expert', [(i, i ^ masks[i % len(masks)]) for i in ra...  6.35 us
    pallas_call x1, Pallas kernels, first_call(): pl.pallas_call(first_kernel, out_shape=tuple((pltpu.VMEM(shape, kind) for...  3.38 us
    pallas_call x1, Pallas kernels, experts_call(): pl.pallas_call(expert_kernel, out_shape=(half, half), in_specs=[VMEM] * (...  2.11 us
    convert_element_type x1, other arithmetic, dense_body(): (own + table[:, 1:2] * cross.astype(jnp.float32)).astype(jnp.bfloat16)  0.72 us
  transfers between devices with their start and end apart: 16, of which 7 were waited for; matrix products, arithmetic and copies ran while one was open for 1% of the time, Pallas kernels for 10%

profile of v5, /device:TPU:0, one launch (start us, length us, event | category | flops | bytes accessed | tf_op | source)
XLA Modules:
  0.0 34.3 jit_solution(15236914793255260757)
XLA Ops:
  0.0 4.0 %collective-permute-start = (bf16[4,7168]{1,0:T(4,128)(2,1)}, bf16[4,7168]{1,0:T(4,128)(2,1)S(1)}, u32[]{:S(2)}, u32[]{:S(2)}) collective-permute-start(bf16[4,7168]{1,0:T(4,128)(2,1)} %refs_3_.1), channel_id=1, source_target_pairs={{0,8},{1,9},{2,10},{3,11},{4,12},{5,13},{6,14},{7,15},{8,0},{9,1},... | collective-permute-start | bytes 172040 | tf_op jit(solution)/shard_map/ppermute | solution.py:62
  4.0 1.5 %collective-permute-start.1 = (bf16[4,7168]{1,0:T(4,128)(2,1)}, bf16[4,7168]{1,0:T(4,128)(2,1)S(1)}, u32[]{:S(2)}, u32[]{:S(2)}) collective-permute-start(bf16[4,7168]{1,0:T(4,128)(2,1)} %refs_3_.1), channel_id=1, source_target_pairs={{0,2},{1,5},{2,0},{3,7},{4,6},{5,1},{6,4},{7,3},{8,10},{9,13},{10,... | collective-permute-start | bytes 172040 | tf_op jit(solution)/shard_map/ppermute | solution.py:62
  5.5 1.6 %collective-permute-start.2 = (bf16[4,7168]{1,0:T(4,128)(2,1)}, bf16[4,7168]{1,0:T(4,128)(2,1)S(1)}, u32[]{:S(2)}, u32[]{:S(2)}) collective-permute-start(bf16[4,7168]{1,0:T(4,128)(2,1)} %refs_3_.1), channel_id=1, source_target_pairs={{0,4},{1,3},{2,6},{3,1},{4,0},{5,7},{6,2},{7,5},{8,12},{9,11},{10,... | collective-permute-start | bytes 172040 | tf_op jit(solution)/shard_map/ppermute | solution.py:62
  7.1 0.4 %collective-permute-start.3 = (bf16[4,7168]{1,0:T(4,128)(2,1)}, bf16[4,7168]{1,0:T(4,128)(2,1)S(1)}, u32[]{:S(2)}, u32[]{:S(2)}) collective-permute-start(bf16[4,7168]{1,0:T(4,128)(2,1)} %refs_3_.1), channel_id=1, source_target_pairs={{0,6},{1,7},{2,4},{3,5},{4,2},{5,3},{6,0},{7,1},{8,14},{9,15},{10,... | collective-permute-start | bytes 172040 | tf_op jit(solution)/shard_map/ppermute | solution.py:62
  7.5 0.0 collective-permute-done.refs_0_
  7.5 1.5 %collective-permute-start.4 = (bf16[4,7168]{1,0:T(4,128)(2,1)S(1)}, bf16[4,7168]{1,0:T(4,128)(2,1)S(1)}, u32[]{:S(2)}, u32[]{:S(2)}) collective-permute-start(bf16[4,7168]{1,0:T(4,128)(2,1)S(1)} %collective-permute-done.refs_0_), channel_id=1, source_target_pairs={{0,2},{1,5},{2,0},{3,7},{4,6},{5,1},{6,4},{7,3},{8,10},{9,13},{10,... | collective-permute-start | bytes 172040 | tf_op jit(solution)/shard_map/ppermute | solution.py:62
  9.0 1.5 %collective-permute-start.5 = (bf16[4,7168]{1,0:T(4,128)(2,1)S(1)}, bf16[4,7168]{1,0:T(4,128)(2,1)S(1)}, u32[]{:S(2)}, u32[]{:S(2)}) collective-permute-start(bf16[4,7168]{1,0:T(4,128)(2,1)S(1)} %collective-permute-done.refs_0_), channel_id=1, source_target_pairs={{0,6},{1,7},{2,4},{3,5},{4,2},{5,3},{6,0},{7,1},{8,14},{9,15},{10,... | collective-permute-start | bytes 172040 | tf_op jit(solution)/shard_map/ppermute | solution.py:62
  10.6 0.0 collective-permute-done.1.refs_1_
  10.6 0.5 %collective-permute-start.6 = (bf16[4,7168]{1,0:T(4,128)(2,1)S(1)}, bf16[4,7168]{1,0:T(4,128)(2,1)S(1)}, u32[]{:S(2)}, u32[]{:S(2)}) collective-permute-start(bf16[4,7168]{1,0:T(4,128)(2,1)S(1)} %collective-permute-done.refs_0_), channel_id=1, source_target_pairs={{0,4},{1,3},{2,6},{3,1},{4,0},{5,7},{6,2},{7,5},{8,12},{9,11},{10,... | collective-permute-start | bytes 172040 | tf_op jit(solution)/shard_map/ppermute | solution.py:62
  11.0 0.0 collective-permute-done.2.refs_2_
  11.0 0.0 copy-start
  11.0 3.4 %shard_map.73 = (bf16[16,7168]{1,0:T(8,128)(2,1)S(1)}, f32[1,7168]{1,0:T(1,128)S(1)}, bf16[1,7168,256]{2,1,0:T(8,128)(2,1)S(1)}, bf16[1,7168,256]{2,1,0:T(8,128)(2,1)S(1)}) custom-call(bf16[4,7168]{1,0:T(4,128)(2,1)S(1)} %collective-permute-done.refs_0_, bf16[4,7168]{1,0:T(4,128)(2,1)S(1)} %collective-permute-done.1.refs_1_, ...), custom_call_target="tpu_custom_call" | custom-call | bytes 14680064 | tf_op jit(solution)/shard_map/pallas_call | solution.py:91
  14.4 0.0 collective-permute-done.3.refs_0_
  14.4 0.0 collective-permute-done.4.refs_1_
  14.4 0.0 collective-permute-done.5.refs_2_
  14.4 0.3 collective-permute-done.6.refs_3_
  14.8 0.3 shard_map.74.refs_0_
  15.0 0.1 collective-permute-start.7
  15.1 1.8 %collective-permute-done.7.refs_1_ = bf16[32,7168]{1,0:T(8,128)(2,1)S(1)} collective-permute-done((bf16[32,7168]{1,0:T(8,128)(2,1)S(1)}, bf16[32,7168]{1,0:T(8,128)(2,1)S(1)}, u32[]{:S(2)}, u32[]{:S(2)}) %collective-permute-start.7) | collective-permute-done | bytes 458784 | tf_op jit(solution)/shard_map/ppermute | solution.py:62
  16.9 0.0 copy-done
  16.9 0.0 copy-start.1
  16.9 0.0 copy-start.2
  16.9 2.1 %shard_map.75 = (bf16[8,4,7168]{2,1,0:T(4,128)(2,1)S(1)}, bf16[8,4,7168]{2,1,0:T(4,128)(2,1)S(1)}) custom-call(bf16[32,7168]{1,0:T(8,128)(2,1)S(1)} %shard_map.74.refs_0_, bf16[32,7168]{1,0:T(8,128)(2,1)S(1)} %collective-permute-done.7.refs_1_, bf16[1,7168,256]{2,1,0:T(8,128)(2,1)S(1)} %get-tuple-element.20.refs_2_, ...), custom_call_target="tpu_custom_call" | custom-call | tf_op jit(solution)/shard_map/pallas_call | solution.py:146
  19.0 0.2 collective-permute-start.8
  19.2 0.1 pad_add_fusion
  19.3 1.6 %collective-permute-done.8.got = bf16[8,4,7168]{2,1,0:T(4,128)(2,1)S(1)} collective-permute-done((bf16[8,4,7168]{2,1,0:T(4,128)(2,1)S(1)}, bf16[8,4,7168]{2,1,0:T(4,128)(2,1)S(1)}, u32[]{:S(2)}, u32[]{:S(2)}) %collective-permute-start.8) | collective-permute-done | bytes 458784 | tf_op jit(solution)/shard_map/ppermute | solution.py:62
  20.9 0.2 shard_map.76
  21.1 1.6 %collective-permute-start.12 = (bf16[4,7168]{1,0:T(4,128)(2,1)S(1)}, bf16[4,7168]{1,0:T(4,128)(2,1)S(1)}, u32[]{:S(2)}, u32[]{:S(2)}) collective-permute-start(bf16[4,7168]{1,0:T(4,128)(2,1)S(1)} %get-tuple-element.28), channel_id=1, source_target_pairs={{0,2},{1,5},{2,0},{3,7},{4,6},{5,1},{6,4},{7,3},{8,10},{9,13},{10,... | collective-permute-start | bytes 172040 | tf_op jit(solution)/shard_map/ppermute | solution.py:62
  22.6 1.3 %collective-permute-start.13 = (bf16[4,7168]{1,0:T(4,128)(2,1)S(1)}, bf16[4,7168]{1,0:T(4,128)(2,1)S(1)}, u32[]{:S(2)}, u32[]{:S(2)}) collective-permute-start(bf16[4,7168]{1,0:T(4,128)(2,1)S(1)} %get-tuple-element.29), channel_id=1, source_target_pairs={{0,6},{1,7},{2,4},{3,5},{4,2},{5,3},{6,0},{7,1},{8,14},{9,15},{10,... | collective-permute-start | bytes 172040 | tf_op jit(solution)/shard_map/ppermute | solution.py:62
  23.9 0.7 %collective-permute-start.14 = (bf16[4,7168]{1,0:T(4,128)(2,1)S(1)}, bf16[4,7168]{1,0:T(4,128)(2,1)S(1)}, u32[]{:S(2)}, u32[]{:S(2)}) collective-permute-start(bf16[4,7168]{1,0:T(4,128)(2,1)S(1)} %get-tuple-element.30), channel_id=1, source_target_pairs={{0,4},{1,3},{2,6},{3,1},{4,0},{5,7},{6,2},{7,5},{8,12},{9,11},{10,... | collective-permute-start | bytes 172040 | tf_op jit(solution)/shard_map/ppermute | solution.py:62
  24.6 0.0 copy-done.1
  24.6 0.0 copy-done.2
  24.6 0.1 fusion
  24.7 1.3 %collective-permute-start.10 = (bf16[4,7168]{1,0:T(4,128)(2,1)S(1)}, bf16[4,7168]{1,0:T(4,128)(2,1)S(1)}, u32[]{:S(2)}, u32[]{:S(2)}) collective-permute-start(bf16[4,7168]{1,0:T(4,128)(2,1)S(1)} %get-tuple-element.25), channel_id=1, source_target_pairs={{0,4},{1,3},{2,6},{3,1},{4,0},{5,7},{6,2},{7,5},{8,12},{9,11},{10,... | collective-permute-start | bytes 172040 | tf_op jit(solution)/shard_map/ppermute | solution.py:62
  26.0 1.7 %collective-permute-start.11 = (bf16[4,7168]{1,0:T(4,128)(2,1)S(1)}, bf16[4,7168]{1,0:T(4,128)(2,1)S(1)}, u32[]{:S(2)}, u32[]{:S(2)}) collective-permute-start(bf16[4,7168]{1,0:T(4,128)(2,1)S(1)} %get-tuple-element.26), channel_id=1, source_target_pairs={{0,6},{1,7},{2,4},{3,5},{4,2},{5,3},{6,0},{7,1},{8,14},{9,15},{10,... | collective-permute-start | bytes 172040 | tf_op jit(solution)/shard_map/ppermute | solution.py:62
  27.7 0.0 collective-permute-done.12.a
  27.7 0.5 %collective-permute-start.9 = (bf16[4,7168]{1,0:T(4,128)(2,1)S(1)}, bf16[4,7168]{1,0:T(4,128)(2,1)S(1)}, u32[]{:S(2)}, u32[]{:S(2)}) collective-permute-start(bf16[4,7168]{1,0:T(4,128)(2,1)S(1)} %get-tuple-element.24), channel_id=1, source_target_pairs={{0,2},{1,5},{2,0},{3,7},{4,6},{5,1},{6,4},{7,3},{8,10},{9,13},{10,... | collective-permute-start | bytes 172040 | tf_op jit(solution)/shard_map/ppermute | solution.py:62
  28.2 0.0 collective-permute-done.13.b
  28.2 0.1 collective-permute-done.14.c
  28.4 2.5 %collective-permute-start.15 = (bf16[4,7168]{1,0:T(4,128)(2,1)S(1)}, bf16[4,7168]{1,0:T(4,128)(2,1)S(1)}, u32[]{:S(2)}, u32[]{:S(2)}) collective-permute-start(bf16[4,7168]{1,0:T(4,128)(2,1)S(1)} %shard_map.78), channel_id=1, source_target_pairs={{0,8},{1,9},{2,10},{3,11},{4,12},{5,13},{6,14},{7,15},{8,0},{9,1},... | collective-permute-start | bytes 172040 | tf_op jit(solution)/shard_map/ppermute | solution.py:62
  30.9 0.1 copy.12.tables
  31.0 0.0 collective-permute-done.10.b
  31.0 0.5 %collective-permute-done.11.c = bf16[4,7168]{1,0:T(4,128)(2,1)S(1)} collective-permute-done((bf16[4,7168]{1,0:T(4,128)(2,1)S(1)}, bf16[4,7168]{1,0:T(4,128)(2,1)S(1)}, u32[]{:S(2)}, u32[]{:S(2)}) %collective-permute-start.11) | collective-permute-done | bytes 57376 | tf_op jit(solution)/shard_map/ppermute | solution.py:62
  31.5 0.6 %collective-permute-done.9.a = bf16[4,7168]{1,0:T(4,128)(2,1)S(1)} collective-permute-done((bf16[4,7168]{1,0:T(4,128)(2,1)S(1)}, bf16[4,7168]{1,0:T(4,128)(2,1)S(1)}, u32[]{:S(2)}, u32[]{:S(2)}) %collective-permute-start.9) | collective-permute-done | bytes 57376 | tf_op jit(solution)/shard_map/ppermute | solution.py:62
  32.1 0.1 shard_map.77
  32.2 1.4 %collective-permute-done.15 = bf16[4,7168]{1,0:T(4,128)(2,1)S(1)} collective-permute-done((bf16[4,7168]{1,0:T(4,128)(2,1)S(1)}, bf16[4,7168]{1,0:T(4,128)(2,1)S(1)}, u32[]{:S(2)}, u32[]{:S(2)}) %collective-permute-start.15) | collective-permute-done | bytes 57376 | tf_op jit(solution)/shard_map/ppermute | solution.py:62
  33.6 0.7 %add_convert_fusion = bf16[4,7168]{1,0:T(4,128)(2,1)} fusion(f32[4,7168]{1,0:T(4,128)S(1)} %shard_map.77, bf16[4,7168]{1,0:T(4,128)(2,1)S(1)} %collective-permute-done.15, f32[4]{0:T(128)S(1)} %slice_bitcast_fusion), kind=kLoop, calls=%fused_computation | loop fusion | flops 114688 | bytes 229392 | tf_op jit(solution)/shard_map/convert_element_type | solution.py:203
  (2 shorter events, 0.0 us)
Async XLA Ops:
  0.0 7.5 %collective-permute-start = (bf16[4,7168]{1,0:T(4,128)(2,1)}, bf16[4,7168]{1,0:T(4,128)(2,1)S(1)}, u32[]{:S(2)}, u32[]{:S(2)}) collective-permute-start(bf16[4,7168]{1,0:T(4,128)(2,1)} %refs_3_.1), channel_id=1, source_target_pairs={{0,8},{1,9},{2,10},{3,11},{4,12},{5,13},{6,14},{7,15},{8,0},{9,1},... | collective-permute-start | bytes 172040 | tf_op jit(solution)/shard_map/ppermute | solution.py:62
  4.0 6.5 %collective-permute-start.1 = (bf16[4,7168]{1,0:T(4,128)(2,1)}, bf16[4,7168]{1,0:T(4,128)(2,1)S(1)}, u32[]{:S(2)}, u32[]{:S(2)}) collective-permute-start(bf16[4,7168]{1,0:T(4,128)(2,1)} %refs_3_.1), channel_id=1, source_target_pairs={{0,2},{1,5},{2,0},{3,7},{4,6},{5,1},{6,4},{7,3},{8,10},{9,13},{10,... | collective-permute-start | bytes 172040 | tf_op jit(solution)/shard_map/ppermute | solution.py:62
  5.5 5.5 %collective-permute-start.2 = (bf16[4,7168]{1,0:T(4,128)(2,1)}, bf16[4,7168]{1,0:T(4,128)(2,1)S(1)}, u32[]{:S(2)}, u32[]{:S(2)}) collective-permute-start(bf16[4,7168]{1,0:T(4,128)(2,1)} %refs_3_.1), channel_id=1, source_target_pairs={{0,4},{1,3},{2,6},{3,1},{4,0},{5,7},{6,2},{7,5},{8,12},{9,11},{10,... | collective-permute-start | bytes 172040 | tf_op jit(solution)/shard_map/ppermute | solution.py:62
  7.1 7.3 %collective-permute-start.3 = (bf16[4,7168]{1,0:T(4,128)(2,1)}, bf16[4,7168]{1,0:T(4,128)(2,1)S(1)}, u32[]{:S(2)}, u32[]{:S(2)}) collective-permute-start(bf16[4,7168]{1,0:T(4,128)(2,1)} %refs_3_.1), channel_id=1, source_target_pairs={{0,6},{1,7},{2,4},{3,5},{4,2},{5,3},{6,0},{7,1},{8,14},{9,15},{10,... | collective-permute-start | bytes 172040 | tf_op jit(solution)/shard_map/ppermute | solution.py:62
  7.5 6.9 %collective-permute-start.4 = (bf16[4,7168]{1,0:T(4,128)(2,1)S(1)}, bf16[4,7168]{1,0:T(4,128)(2,1)S(1)}, u32[]{:S(2)}, u32[]{:S(2)}) collective-permute-start(bf16[4,7168]{1,0:T(4,128)(2,1)S(1)} %collective-permute-done.refs_0_), channel_id=1, source_target_pairs={{0,2},{1,5},{2,0},{3,7},{4,6},{5,1},{6,4},{7,3},{8,10},{9,13},{10,... | collective-permute-start | bytes 172040 | tf_op jit(solution)/shard_map/ppermute | solution.py:62
  9.0 5.4 %collective-permute-start.5 = (bf16[4,7168]{1,0:T(4,128)(2,1)S(1)}, bf16[4,7168]{1,0:T(4,128)(2,1)S(1)}, u32[]{:S(2)}, u32[]{:S(2)}) collective-permute-start(bf16[4,7168]{1,0:T(4,128)(2,1)S(1)} %collective-permute-done.refs_0_), channel_id=1, source_target_pairs={{0,6},{1,7},{2,4},{3,5},{4,2},{5,3},{6,0},{7,1},{8,14},{9,15},{10,... | collective-permute-start | bytes 172040 | tf_op jit(solution)/shard_map/ppermute | solution.py:62
  10.6 4.2 %collective-permute-start.6 = (bf16[4,7168]{1,0:T(4,128)(2,1)S(1)}, bf16[4,7168]{1,0:T(4,128)(2,1)S(1)}, u32[]{:S(2)}, u32[]{:S(2)}) collective-permute-start(bf16[4,7168]{1,0:T(4,128)(2,1)S(1)} %collective-permute-done.refs_0_), channel_id=1, source_target_pairs={{0,4},{1,3},{2,6},{3,1},{4,0},{5,7},{6,2},{7,5},{8,12},{9,11},{10,... | collective-permute-start | bytes 172040 | tf_op jit(solution)/shard_map/ppermute | solution.py:62
  11.0 5.9 %copy-start = (bf16[1,256,7168]{2,1,0:T(8,128)(2,1)S(1)}, bf16[1,256,7168]{2,1,0:T(8,128)(2,1)}, u32[]{:S(2)}) copy-start(bf16[1,256,7168]{2,1,0:T(8,128)(2,1)} %refs_4_.1) | copy-start | bytes 11010052
  15.0 1.9 %collective-permute-start.7 = (bf16[32,7168]{1,0:T(8,128)(2,1)S(1)}, bf16[32,7168]{1,0:T(8,128)(2,1)S(1)}, u32[]{:S(2)}, u32[]{:S(2)}) collective-permute-start(bf16[32,7168]{1,0:T(8,128)(2,1)S(1)} %shard_map.74.refs_0_), channel_id=1, source_target_pairs={{0,1},{1,0},{2,3},{3,2},{4,5},{5,4},{6,7},{7,6},{8,9},{9,8},{10,11... | collective-permute-start | bytes 1376264 | tf_op jit(solution)/shard_map/ppermute | solution.py:62
  16.9 7.7 %copy-start.1 = (f32[4,2]{0,1:T(2,128)S(1)}, f32[4,2]{0,1:T(2,128)}, u32[]{:S(2)}) copy-start(f32[4,2]{0,1:T(2,128)} %param.10) | copy-start | bytes 100
  16.9 7.7 %copy-start.2 = (s32[4,2]{0,1:T(2,128)S(1)}, s32[4,2]{0,1:T(2,128)}, u32[]{:S(2)}) copy-start(s32[4,2]{0,1:T(2,128)} %param.9) | copy-start | bytes 100
  19.0 1.9 %collective-permute-start.8 = (bf16[8,4,7168]{2,1,0:T(4,128)(2,1)S(1)}, bf16[8,4,7168]{2,1,0:T(4,128)(2,1)S(1)}, u32[]{:S(2)}, u32[]{:S(2)}) collective-permute-start(bf16[8,4,7168]{2,1,0:T(4,128)(2,1)S(1)} %get-tuple-element.23), channel_id=1, source_target_pairs={{0,1},{1,0},{2,3},{3,2},{4,5},{5,4},{6,7},{7,6},{8,9},{9,8},{10,11... | collective-permute-start | bytes 1376264 | tf_op jit(solution)/shard_map/ppermute | solution.py:62
  21.1 6.6 %collective-permute-start.12 = (bf16[4,7168]{1,0:T(4,128)(2,1)S(1)}, bf16[4,7168]{1,0:T(4,128)(2,1)S(1)}, u32[]{:S(2)}, u32[]{:S(2)}) collective-permute-start(bf16[4,7168]{1,0:T(4,128)(2,1)S(1)} %get-tuple-element.28), channel_id=1, source_target_pairs={{0,2},{1,5},{2,0},{3,7},{4,6},{5,1},{6,4},{7,3},{8,10},{9,13},{10,... | collective-permute-start | bytes 172040 | tf_op jit(solution)/shard_map/ppermute | solution.py:62
  22.6 5.6 %collective-permute-start.13 = (bf16[4,7168]{1,0:T(4,128)(2,1)S(1)}, bf16[4,7168]{1,0:T(4,128)(2,1)S(1)}, u32[]{:S(2)}, u32[]{:S(2)}) collective-permute-start(bf16[4,7168]{1,0:T(4,128)(2,1)S(1)} %get-tuple-element.29), channel_id=1, source_target_pairs={{0,6},{1,7},{2,4},{3,5},{4,2},{5,3},{6,0},{7,1},{8,14},{9,15},{10,... | collective-permute-start | bytes 172040 | tf_op jit(solution)/shard_map/ppermute | solution.py:62
  23.9 4.5 %collective-permute-start.14 = (bf16[4,7168]{1,0:T(4,128)(2,1)S(1)}, bf16[4,7168]{1,0:T(4,128)(2,1)S(1)}, u32[]{:S(2)}, u32[]{:S(2)}) collective-permute-start(bf16[4,7168]{1,0:T(4,128)(2,1)S(1)} %get-tuple-element.30), channel_id=1, source_target_pairs={{0,4},{1,3},{2,6},{3,1},{4,0},{5,7},{6,2},{7,5},{8,12},{9,11},{10,... | collective-permute-start | bytes 172040 | tf_op jit(solution)/shard_map/ppermute | solution.py:62
  24.7 6.3 %collective-permute-start.10 = (bf16[4,7168]{1,0:T(4,128)(2,1)S(1)}, bf16[4,7168]{1,0:T(4,128)(2,1)S(1)}, u32[]{:S(2)}, u32[]{:S(2)}) collective-permute-start(bf16[4,7168]{1,0:T(4,128)(2,1)S(1)} %get-tuple-element.25), channel_id=1, source_target_pairs={{0,4},{1,3},{2,6},{3,1},{4,0},{5,7},{6,2},{7,5},{8,12},{9,11},{10,... | collective-permute-start | bytes 172040 | tf_op jit(solution)/shard_map/ppermute | solution.py:62
  26.0 5.5 %collective-permute-start.11 = (bf16[4,7168]{1,0:T(4,128)(2,1)S(1)}, bf16[4,7168]{1,0:T(4,128)(2,1)S(1)}, u32[]{:S(2)}, u32[]{:S(2)}) collective-permute-start(bf16[4,7168]{1,0:T(4,128)(2,1)S(1)} %get-tuple-element.26), channel_id=1, source_target_pairs={{0,6},{1,7},{2,4},{3,5},{4,2},{5,3},{6,0},{7,1},{8,14},{9,15},{10,... | collective-permute-start | bytes 172040 | tf_op jit(solution)/shard_map/ppermute | solution.py:62
  27.7 4.4 %collective-permute-start.9 = (bf16[4,7168]{1,0:T(4,128)(2,1)S(1)}, bf16[4,7168]{1,0:T(4,128)(2,1)S(1)}, u32[]{:S(2)}, u32[]{:S(2)}) collective-permute-start(bf16[4,7168]{1,0:T(4,128)(2,1)S(1)} %get-tuple-element.24), channel_id=1, source_target_pairs={{0,2},{1,5},{2,0},{3,7},{4,6},{5,1},{6,4},{7,3},{8,10},{9,13},{10,... | collective-permute-start | bytes 172040 | tf_op jit(solution)/shard_map/ppermute | solution.py:62
  28.4 5.2 %collective-permute-start.15 = (bf16[4,7168]{1,0:T(4,128)(2,1)S(1)}, bf16[4,7168]{1,0:T(4,128)(2,1)S(1)}, u32[]{:S(2)}, u32[]{:S(2)}) collective-permute-start(bf16[4,7168]{1,0:T(4,128)(2,1)S(1)} %shard_map.78), channel_id=1, source_target_pairs={{0,8},{1,9},{2,10},{3,11},{4,12},{5,13},{6,14},{7,15},{8,0},{9,1},... | collective-permute-start | bytes 172040 | tf_op jit(solution)/shard_map/ppermute | solution.py:62
